TPU v7x, 128 devices: a whole 4x4x4 slice. The times are simulated.
128 devices in a mesh: grp: 4 (over y), sub: 32 (over z, x, core).
Axes of the slice: x: 4, y: 4, z: 4, core: 2. Of those that a mesh axis runs over, the one named last changes fastest.
Arguments:
- pulses: bfloat16 [4, 32, 128, 32768], P('grp', None, None, 'sub'), may hold values from -6 to 6
- footprint: int32 [32, 2], replicated, may hold values from 0 to 31, as said below
- proj_weight: bfloat16 [32, 48, 256], replicated, may hold values from -0.375 to 0.375
- bank: bfloat16 [8, 512, 512], replicated, may hold values from -0.1875 to 0.1875
- merge_index: int32 [3, 4, 32, 64, 2], P(None, 'grp'), may hold values from 0 to 7
Outputs:
- slab: bfloat16 [1536, 32768], P('sub', 'grp')
Inputs may be any that keep to these rules, and one draw needn't show every extreme that they name: `footprint`: owner o's first entry is block o; its second is another block, different from o.
All inputs are finite; a program needn't handle non-finite values.
Results may differ from a plain program's by a relative error of at most 0.0064.
Values may be sent and summed in bfloat16 or wider, within the bound.
No kernel may reach another device: no remote copies, remote signals or barrier semaphores. Data moves between devices by JAX's collectives and lax.ppermute only.
A program may use at most 256 MiB of HBM per device.

v0:
```python
import jax
import jax.numpy as jnp
from jax import lax
from jax.sharding import PartitionSpec as P


def from_partner(value, axis, stride):
    mask = 2**stride
    pairs = [(source, source ^ mask) for source in range(lax.axis_size(axis))]
    return lax.ppermute(value, axis, pairs)


def body(pulses, footprint, proj_weight, bank, merge_index):
    owners = lax.axis_size("sub")
    position = lax.axis_index("sub")
    held_pulses = pulses[0]
    picked = jnp.take(held_pulses, footprint.reshape(-1), axis=0)
    pulse_rows = picked.reshape(
        owners, footprint.shape[1] * held_pulses.shape[1], held_pulses.shape[2]
    )
    group_table = merge_index[:, 0]
    level_count = group_table.shape[0]
    block_width = bank.shape[1]
    arrived = lax.all_to_all(pulse_rows, "sub", split_axis=0, concat_axis=2, tiled=True)
    weight = lax.dynamic_index_in_dim(proj_weight, position, 0, keepdims=False)
    current = jnp.dot(weight, arrived[0], preferred_element_type=jnp.float32).astype(jnp.bfloat16)
    index_table = lax.dynamic_index_in_dim(group_table, position, 1, keepdims=False)
    beam_count = current.shape[0]
    block_count = current.shape[1] // block_width
    for section_level in range(level_count):
        partner_image = from_partner(current, "sub", section_level)
        self_mats = jnp.take(bank, index_table[section_level, :, 0], axis=0)
        merged = jnp.einsum(
            "sbk,bkj->sbj",
            current.reshape(beam_count, block_count, block_width),
            self_mats,
            preferred_element_type=jnp.float32,
        )
        cross_mats = jnp.take(bank, index_table[section_level, :, 1], axis=0)
        merged = merged + jnp.einsum(
            "sbk,bkj->sbj",
            partner_image.reshape(beam_count, block_count, block_width),
            cross_mats,
            preferred_element_type=jnp.float32,
        )
        merged = merged.reshape(beam_count, block_count * block_width)
        if section_level + 1 < level_count:
            current = merged.astype(jnp.bfloat16)
        else:
            current = merged
    summed = lax.psum_scatter(current, "grp", scatter_dimension=1, tiled=True)
    return summed.astype(jnp.bfloat16)


def solution(mesh):
    placed = (P("grp", None, None, "sub"), P(), P(), P(), P(None, "grp", None, None, None))
    return jax.shard_map(
        body, mesh=mesh, in_specs=placed, out_specs=P("sub", "grp"), check_vma=False
    )
```

profile of v0, /device:TPU:1, one launch (start us, length us, event | category | flops | bytes accessed | tf_op | source)
XLA Modules:
  0.0 609.3 jit_solution(6896463822603979755)
XLA Ops:
  8.4 11.0 %gather_fusion = bf16[64,128,1024]{2,1,0:T(8,128)(2,1)} fusion(bf16[32,128,1024]{2,1,0:T(8,128)(2,1)} %bitcast.88, s32[1024]{0:T(1024)S(1)} %pad_clamp_fusion.6), kind=kCustom, calls=%fused_computation.6 | custom fusion | bytes 33554688 | tf_op jit(solution)/shard_map/jit(_take)/gather | solution.py:17
  19.4 14.2 %bitcast_select_fusion = bf16[32,256,1024]{2,1,0:T(8,128)(2,1)} fusion(pred[32,256]{1,0:T(8,128)(4,1)S(1)} %bitcast.94, bf16[32,256,1024]{2,1,0:T(8,128)(2,1)} %bitcast.87), kind=kLoop, calls=%fused_computation.26 | loop fusion | flops 8388608 | bytes 33562624 | tf_op jit(solution)/shard_map/jit(_take)/select_n | solution.py:17
  33.6 9.5 %all-to-all-start = ((bf16[32,256,1024]{2,1,0:T(8,128)(2,1)}), bf16[32,256,1024]{2,1,0:T(8,128)(2,1)}, u32[]{:S(2)}, u32[]{:S(2)}) async-start(bf16[32,256,1024]{2,1,0:T(8,128)(2,1)} %bitcast_select_fusion), calls=%async_computation | async-start | bytes 33554432 | tf_op jit(solution)/shard_map/all_to_all | solution.py:24
  43.2 201.9 %all-to-all-done = bf16[32,256,1024]{2,1,0:T(8,128)(2,1)} async-done(((bf16[32,256,1024]{2,1,0:T(8,128)(2,1)}), bf16[32,256,1024]{2,1,0:T(8,128)(2,1)}, u32[]{:S(2)}, u32[]{:S(2)}) %all-to-all-start) | async-done | bytes 16777248 | tf_op jit(solution)/shard_map/all_to_all | solution.py:24
  245.0 22.5 %copy.21 = bf16[1,256,32,1024]{1,3,2,0:T(8,128)(2,1)} copy(bf16[1,256,32,1024]{3,1,2,0:T(8,128)(2,1)} %bitcast.9) | data formatting | bytes 33554432 | tf_op jit(solution)/shard_map/all_to_all | solution.py:24
  267.5 12.4 %convolution_convert_fusion = bf16[48,32768]{1,0:T(8,128)(2,1)} fusion(bf16[256,32768]{0,1:T(8,128)(2,1)} %bitcast.86, bf16[32,48,256]{2,1,0:T(8,128)(2,1)S(1)} %copy-done, s32[]{:T(128)S(6)} %select_n.34), kind=kOutput, calls=%fused_computation.7 | convolution fusion | flops 806879232 | bytes 19947524 | tf_op jit(solution)/shard_map/dot_general | solution.py:26
  280.0 11.6 %collective-permute-start = (bf16[48,32768]{1,0:T(8,128)(2,1)}, bf16[48,32768]{1,0:T(8,128)(2,1)}, u32[]{:S(2)}, u32[]{:S(2)}) collective-permute-start(bf16[48,32768]{1,0:T(8,128)(2,1)} %convolution_convert_fusion), channel_id=1, source_target_pairs={{0,1},{1,0},{2,3},{3,2},{4,5},{5,4},{6,7},{7,6},{8,9},{9,8},{10,11... | collective-permute-start | bytes 9437192 | tf_op jit(solution)/shard_map/ppermute | solution.py:10
  292.8 14.7 %gather_fusion.3 = bf16[64,512,512]{2,1,0:T(8,128)(2,1)} fusion(bf16[8,512,512]{2,1,0:T(8,128)(2,1)} %param.10, s32[1024]{0:T(1024)S(1)} %pad_clamp_fusion.5), kind=kCustom, calls=%fused_computation.2.clone | custom fusion | bytes 67109120 | tf_op jit(solution)/shard_map/jit(_take)/gather | solution.py:32
  307.5 14.5 %gather_fusion.4 = bf16[64,512,512]{2,1,0:T(8,128)(2,1)} fusion(bf16[8,512,512]{2,1,0:T(8,128)(2,1)} %param.10, s32[1024]{0:T(1024)S(1)} %get-tuple-element.29), kind=kCustom, calls=%fused_computation.3.clone | custom fusion | bytes 67109120 | tf_op jit(solution)/shard_map/jit(_take)/gather | solution.py:39
  322.0 17.6 %fusion.6 = f32[64,512,48]{1,2,0:T(8,128)} fusion(bf16[64,512,512]{2,1,0:T(8,128)(2,1)} %gather_fusion.3, pred[64]{0:T(512)(128)(4,1)S(1)} %get-tuple-element.22, bf16[6,64,8,512]{3,2,1,0:T(8,128)(2,1)} %bitcast.90), kind=kOutput, calls=%fused_computation.14 | convolution fusion | flops 1627389952 | bytes 42991680 | tf_op jit(solution)/shard_map/sbk,bkj->sbj/dot_general | solution.py:33
  339.7 15.6 %add_convert_fusion.1 = bf16[64,512,48]{1,2,0:T(8,128)(2,1)S(1)} fusion(f32[64,512,48]{1,2,0:T(8,128)} %fusion.6, bf16[64,512,512]{2,1,0:T(8,128)(2,1)} %gather_fusion.4, pred[64]{0:T(512)(128)(4,1)S(1)} %get-tuple-element.20, bf16[6,64,8,512]{3,2,1,0:T(8,128)(2,1)} %bitcast.20), kind=kOutput, calls=%fused_computation.35 | convolution fusion | flops 1630535680 | bytes 46137408 | tf_op jit(solution)/shard_map/sbk,bkj->sbj/dot_general | solution.py:40
  358.9 14.7 %gather_fusion.2 = bf16[64,512,512]{2,1,0:T(8,128)(2,1)} fusion(bf16[8,512,512]{2,1,0:T(8,128)(2,1)} %param.10, s32[1024]{0:T(1024)S(1)} %get-tuple-element.28), kind=kCustom, calls=%fused_computation.1.clone | custom fusion | bytes 67109120 | tf_op jit(solution)/shard_map/jit(_take)/gather | solution.py:32
  373.6 14.5 %gather_fusion.5 = bf16[64,512,512]{2,1,0:T(8,128)(2,1)} fusion(bf16[8,512,512]{2,1,0:T(8,128)(2,1)} %param.10, s32[1024]{0:T(1024)S(1)} %pad_clamp_fusion.2), kind=kCustom, calls=%fused_computation.4.clone | custom fusion | bytes 67109120 | tf_op jit(solution)/shard_map/jit(_take)/gather | solution.py:39
  388.2 18.0 %fusion.8 = f32[64,512,48]{1,2,0:T(8,128)} fusion(bf16[64,512,512]{2,1,0:T(8,128)(2,1)} %gather_fusion.2, pred[64]{0:T(512)(128)(4,1)S(1)} %get-tuple-element.24, bf16[64,512,48]{1,2,0:T(8,128)(2,1)} %copy-done.3), kind=kOutput, calls=%fused_computation.16 | convolution fusion | flops 1627389952 | bytes 42991680 | tf_op jit(solution)/shard_map/sbk,bkj->sbj/dot_general | solution.py:33
  406.2 22.9 %collective-permute-done.1 = bf16[48,32768]{1,0:T(8,128)(2,1)} collective-permute-done((bf16[48,32768]{1,0:T(8,128)(2,1)}, bf16[48,32768]{1,0:T(8,128)(2,1)}, u32[]{:S(2)}, u32[]{:S(2)}) %collective-permute-start.1) | collective-permute-done | bytes 3145760 | tf_op jit(solution)/shard_map/ppermute | solution.py:10
  429.0 15.6 %add_convert_fusion = bf16[64,512,48]{1,2,0:T(8,128)(2,1)S(1)} fusion(f32[64,512,48]{1,2,0:T(8,128)} %fusion.8, bf16[64,512,512]{2,1,0:T(8,128)(2,1)} %gather_fusion.5, pred[64]{0:T(512)(128)(4,1)S(1)} %get-tuple-element.18, bf16[6,64,8,512]{3,2,1,0:T(8,128)(2,1)} %bitcast.22), kind=kOutput, calls=%fused_computation.34 | convolution fusion | flops 1630535680 | bytes 46137408 | tf_op jit(solution)/shard_map/sbk,bkj->sbj/dot_general | solution.py:40
  448.3 14.5 %gather_fusion.1 = bf16[64,512,512]{2,1,0:T(8,128)(2,1)} fusion(bf16[8,512,512]{2,1,0:T(8,128)(2,1)} %param.10, s32[1024]{0:T(1024)S(1)} %pad_clamp_fusion.1), kind=kCustom, calls=%fused_computation.clone | custom fusion | bytes 67109120 | tf_op jit(solution)/shard_map/jit(_take)/gather | solution.py:32
  462.9 14.5 %gather_fusion.6 = bf16[64,512,512]{2,1,0:T(8,128)(2,1)} fusion(bf16[8,512,512]{2,1,0:T(8,128)(2,1)} %param.10, s32[1024]{0:T(1024)S(1)} %pad_clamp_fusion), kind=kCustom, calls=%fused_computation.5.clone | custom fusion | bytes 67109120 | tf_op jit(solution)/shard_map/jit(_take)/gather | solution.py:39
  477.3 18.0 %fusion.10 = f32[64,512,48]{1,2,0:T(8,128)} fusion(bf16[64,512,512]{2,1,0:T(8,128)(2,1)} %gather_fusion.1, pred[64]{0:T(512)(128)(4,1)S(1)} %copy-done.7, bf16[64,512,48]{1,2,0:T(8,128)(2,1)} %copy-done.2), kind=kOutput, calls=%fused_computation.18 | convolution fusion | flops 1627389952 | bytes 42991680 | tf_op jit(solution)/shard_map/sbk,bkj->sbj/dot_general | solution.py:33
  495.3 23.7 %collective-permute-done.2 = bf16[48,32768]{1,0:T(8,128)(2,1)} collective-permute-done((bf16[48,32768]{1,0:T(8,128)(2,1)}, bf16[48,32768]{1,0:T(8,128)(2,1)}, u32[]{:S(2)}, u32[]{:S(2)}) %collective-permute-start.2) | collective-permute-done | bytes 3145760 | tf_op jit(solution)/shard_map/ppermute | solution.py:10
  519.0 15.5 %add_bitcast_fusion = f32[64,6,8,512]{3,2,1,0:T(8,128)S(1)} fusion(f32[64,512,48]{1,2,0:T(8,128)} %fusion.10, bf16[64,512,512]{2,1,0:T(8,128)(2,1)} %gather_fusion.6, pred[64]{0:T(512)(128)(4,1)S(1)} %copy-done.6, bf16[6,64,8,512]{3,2,1,0:T(8,128)(2,1)} %bitcast.24), kind=kOutput, calls=%fused_computation.33 | convolution fusion | flops 1628962816 | bytes 49283136 | tf_op jit(solution)/shard_map/sbk,bkj->sbj/dot_general | solution.py:40
  534.6 3.4 copy.35
  538.0 62.1 %reduce-scatter.2.cloned.1.call-done = f32[48,8192]{1,0:T(8,128)} async-done(((f32[48,32768]{1,0:T(8,128)}), f32[48,8192]{1,0:T(8,128)}) %reduce-scatter.2.cloned.1.call-update) | async-done | bytes 1572880 | tf_op jit(solution)/shard_map/reduce_scatter | solution.py:51
  600.0 2.4 convert_element_type.35
  (38 shorter events, 10.6 us)
Async XLA Ops:
  6.5 261.0 %copy-start = (bf16[32,48,256]{2,1,0:T(8,128)(2,1)S(1)}, bf16[32,48,256]{2,1,0:T(8,128)(2,1)}, u32[]{:S(2)}) copy-start(bf16[32,48,256]{2,1,0:T(8,128)(2,1)} %param.9) | copy-start | bytes 2359300
  33.6 211.4 %all-to-all-start = ((bf16[32,256,1024]{2,1,0:T(8,128)(2,1)}), bf16[32,256,1024]{2,1,0:T(8,128)(2,1)}, u32[]{:S(2)}, u32[]{:S(2)}) async-start(bf16[32,256,1024]{2,1,0:T(8,128)(2,1)} %bitcast_select_fusion), calls=%async_computation | async-start | bytes 33554432 | tf_op jit(solution)/shard_map/all_to_all | solution.py:24
  43.1 556.9 %reduce-scatter.2.cloned.1.call-start = ((), (), s32[]{:S(2)}) async-start(), calls=%async_computation.2 | async-start | bytes 7864320 | tf_op jit(solution)/shard_map/reduce_scatter | solution.py:51
  280.0 59.7 %collective-permute-start = (bf16[48,32768]{1,0:T(8,128)(2,1)}, bf16[48,32768]{1,0:T(8,128)(2,1)}, u32[]{:S(2)}, u32[]{:S(2)}) collective-permute-start(bf16[48,32768]{1,0:T(8,128)(2,1)} %convolution_convert_fusion), channel_id=1, source_target_pairs={{0,1},{1,0},{2,3},{3,2},{4,5},{5,4},{6,7},{7,6},{8,9},{9,8},{10,11... | collective-permute-start | bytes 9437192 | tf_op jit(solution)/shard_map/ppermute | solution.py:10
  355.3 1.7 copy-start.3
  358.9 70.1 %collective-permute-start.1 = (bf16[48,32768]{1,0:T(8,128)(2,1)}, bf16[48,32768]{1,0:T(8,128)(2,1)}, u32[]{:S(2)}, u32[]{:S(2)}) collective-permute-start(bf16[48,32768]{1,0:T(8,128)(2,1)} %bitcast.27), channel_id=1, source_target_pairs={{0,2},{1,3},{2,0},{3,1},{4,6},{5,7},{6,4},{7,5},{8,10},{9,11},{10,... | collective-permute-start | bytes 9437192 | tf_op jit(solution)/shard_map/ppermute | solution.py:10
  429.0 19.3 %copy-start.5 = (s32[64]{0:T(128)S(1)}, s32[64]{0:T(128)}, u32[]{:S(2)}) copy-start(s32[64]{0:T(128)} %get-tuple-element.27) | copy-start | bytes 772
  444.6 1.7 copy-start.2
  448.3 70.7 %collective-permute-start.2 = (bf16[48,32768]{1,0:T(8,128)(2,1)}, bf16[48,32768]{1,0:T(8,128)(2,1)}, u32[]{:S(2)}, u32[]{:S(2)}) collective-permute-start(bf16[48,32768]{1,0:T(8,128)(2,1)} %bitcast.29), channel_id=1, source_target_pairs={{0,4},{1,5},{2,6},{3,7},{4,0},{5,1},{6,2},{7,3},{8,12},{9,13},{10,... | collective-permute-start | bytes 9437192 | tf_op jit(solution)/shard_map/ppermute | solution.py:10
  448.3 14.5 %copy-start.4 = (s32[64]{0:T(128)S(1)}, s32[64]{0:T(128)}, u32[]{:S(2)}) copy-start(s32[64]{0:T(128)} %get-tuple-element.7) | copy-start | bytes 772
  462.9 14.5 %copy-start.7 = (pred[64]{0:T(512)(128)(4,1)S(1)}, pred[64]{0:T(512)(128)(4,1)}, u32[]{:S(2)}) copy-start(pred[64]{0:T(512)(128)(4,1)} %get-tuple-element.26) | copy-start | bytes 196
  477.3 41.7 %copy-start.6 = (pred[64]{0:T(512)(128)(4,1)S(1)}, pred[64]{0:T(512)(128)(4,1)}, u32[]{:S(2)}) copy-start(pred[64]{0:T(512)(128)(4,1)} %get-tuple-element.6) | copy-start | bytes 196
  519.0 83.4 %copy-start.1 = (bf16[32,48,256]{2,1,0:T(8,128)(2,1)S(1)}, bf16[32,48,256]{2,1,0:T(8,128)(2,1)}, u32[]{:S(2)}) copy-start(bf16[32,48,256]{2,1,0:T(8,128)(2,1)} %param.9) | copy-start | bytes 2359300
Sparse Core Ops, SparseCore 0:
  538.1 61.9 reduce-scatter.1
where the time goes:
time: 610 us; the launch traced here: 609 us
  waiting for transfers between devices  310 us (51%)
  local copies, waits for them, and re-layouts  134 us (22%)
  matrix products  113 us (19%)
  starting transfers between devices  21.1 us (3%)
  other arithmetic  17.9 us (3%)
  between operations  13.5 us (2%)
    all_to_all x1, waiting for transfers between devices, body(): lax.all_to_all(pulse_rows, 'sub', split_axis=0, concat_axis=2, tiled=True)  202 us
    reduce_scatter x1, waiting for transfers between devices, body(): summed = lax.psum_scatter(current, 'grp', scatter_dimension=1, tiled=True)  62.1 us
    dot_general x3, matrix products, body(): jnp.einsum('sbk,bkj->sbj', current.reshape(beam_count, block_count, block...  53.6 us
    dot_general x3, matrix products, body(): jnp.einsum('sbk,bkj->sbj', partner_image.reshape(beam_count, block_count,...  46.7 us
    ppermute x3, waiting for transfers between devices, from_partner(): return lax.ppermute(value, axis, pairs)  46.5 us
    gather x3, local copies, waits for them, and re-layouts, body(): self_mats = jnp.take(bank, index_table[section_level, :, 0], axis=0)  43.9 us
    gather x3, local copies, waits for them, and re-layouts, body(): cross_mats = jnp.take(bank, index_table[section_level, :, 1], axis=0)  43.5 us
    all_to_all x1, local copies, waits for them, and re-layouts, body(): lax.all_to_all(pulse_rows, 'sub', split_axis=0, concat_axis=2, tiled=True)  22.5 us
  transfers between devices with their start and end apart: 5, of which 4 were waited for; matrix products, arithmetic and copies ran while one was open for 23% of the time, Pallas kernels for 0%

commit v1 on v0

v1 whole, which is shorter than its diff:
```python
import functools
import jax
import jax.numpy as jnp
from jax import lax
from jax.sharding import PartitionSpec as P
from jax.experimental import pallas as pl
from jax.experimental.pallas import tpu as pltpu

def merge_tree(levels, blocks, pick_ref, foot_ref, table_ref, pulses_ref, w0_ref, w1_ref, bank_ref,
               out0_ref, out1_ref, rows, mats, image, row_sem, mat_sem):
    step = pl.program_id(0)
    steps = pl.num_programs(0)
    w_refs, out_refs = (w0_ref, w1_ref), (out0_ref, out1_ref)
    members = w0_ref.shape[0]
    beams = w0_ref.shape[1]
    pulse_block = pulses_ref.shape[1]
    width = bank_ref.shape[1]
    owners = foot_ref.shape[0] // 2

    def fetches(at, slot):
        copies = []
        for b in range(blocks):
            for j in range(members):
                owner = pick_ref[at * blocks + b] * members + j
                for h in range(2):
                    copies.append(pltpu.make_async_copy(
                        pulses_ref.at[foot_ref[owner * 2 + h], :, pl.ds(b * width, width)],
                        rows.at[slot, b, j, pl.ds(h * pulse_block, pulse_block), :],
                        row_sem.at[slot, b, j, h]))
        return copies

    bank_copies = [pltpu.make_async_copy(bank_ref.at[k], mats.at[k], mat_sem.at[k]) for k in range(bank_ref.shape[0])]

    @pl.when(step == 0)
    def _():
        for c in fetches(0, 0):
            c.start()
        for c in bank_copies:
            c.start()

    slot = lax.rem(step, 2)

    @pl.when(step + 1 < steps)
    def _():
        for c in fetches(step + 1, 1 - slot):
            c.start()

    for c in fetches(step, slot):
        c.wait()
    for b in range(blocks):
        for j in range(members):
            image[0, b, j] = jnp.dot(w_refs[b][j], rows[slot, b, j], preferred_element_type=jnp.float32).astype(jnp.bfloat16)

    @pl.when(step == 0)
    def _():
        for c in bank_copies:
            c.wait()

    for level in range(levels):
        now, later = level % 2, (level + 1) % 2
        for b in range(blocks):
            for j in range(members):
                owner = pick_ref[step * blocks + b] * members + j
                at = ((level * owners + owner) * blocks + b) * 2
                acc = jnp.dot(image[now, b, j], mats[table_ref[at]], preferred_element_type=jnp.float32)
                acc = acc + jnp.dot(image[now, b, j ^ (1 << level)], mats[table_ref[at + 1]], preferred_element_type=jnp.float32)
                if level + 1 < levels:
                    image[later, b, j] = acc.astype(jnp.bfloat16)
                else:
                    out_refs[b][j % 4, 0, pl.ds((j // 4) * beams, beams), :] = acc.astype(jnp.bfloat16)


def images_of(pulses, foot, table, weight, bank, pick, levels, members=8):
    steps = pick.shape[0] // 2
    kb, width, _ = bank.shape
    owners, beams, depth = weight.shape
    blocks = pulses.shape[2] // width
    wspec = lambda b: pl.BlockSpec((members, beams, depth), lambda i, pk, ft, tb: (pk[i * blocks + b], 0, 0))
    ospec = pl.BlockSpec((4, 1, members // 4 * beams, width), lambda i, pk, ft, tb: (0, i, 0, 0))
    return pl.pallas_call(
        functools.partial(merge_tree, levels, blocks),
        grid_spec=pltpu.PrefetchScalarGridSpec(
            num_scalar_prefetch=3,
            grid=(steps,),
            in_specs=[pl.BlockSpec(memory_space=pl.ANY), wspec(0), wspec(1), pl.BlockSpec(memory_space=pl.ANY)],
            out_specs=[ospec, ospec],
            scratch_shapes=[
                pltpu.VMEM((2, blocks, members, depth, width), jnp.bfloat16),
                pltpu.VMEM((kb, width, width), jnp.bfloat16),
                pltpu.VMEM((2, blocks, members, beams, width), jnp.bfloat16),
                pltpu.SemaphoreType.DMA((2, blocks, members, 2)),
                pltpu.SemaphoreType.DMA((kb,)),
            ]),
        out_shape=[jax.ShapeDtypeStruct((4, steps, members // 4 * beams, width), jnp.bfloat16)] * 2,
        compiler_params=pltpu.CompilerParams(vmem_limit_bytes=40 * 2**20),
        cost_estimate=pl.CostEstimate(flops=int(steps * 2.8e9), bytes_accessed=steps * 7 * 2**20, transcendentals=0),
    )(pick, foot, table, pulses, weight, weight, bank)


def body(pulses, footprint, proj_weight, bank, merge_index):
    position = lax.axis_index("sub")
    width = bank.shape[1]
    owners, beams, _ = proj_weight.shape
    held = pulses[0]
    blocks = held.shape[2] // width
    levels = merge_index.shape[0]
    table = lax.dynamic_slice_in_dim(merge_index[:, 0], position * blocks, blocks, axis=2).reshape(-1)
    groups = lax.axis_size("grp")
    pick = jnp.repeat(jnp.arange(groups, dtype=jnp.int32), blocks)
    parts = images_of(held, footprint.reshape(-1), table, proj_weight, bank, pick, levels)
    cores = 8
    planes = owners // cores
    rows_of = [[start + i for i in range(cores)] for start in range(0, owners, cores)]
    lines_of = [[start + i * cores for i in range(planes)] for start in range(cores)]
    done = []
    for part in parts:
        summed = lax.psum_scatter(part, "grp", scatter_dimension=0, tiled=True)
        spread = lax.all_to_all(summed[0], "sub", 0, 0, axis_index_groups=lines_of, tiled=True)
        turned = lax.all_to_all(spread, "grp", 0, 0, tiled=True)
        by_owner = turned.reshape(groups, 2, beams, width).transpose(1, 0, 2, 3).reshape(cores, beams, width)
        done.append(lax.all_to_all(by_owner, "sub", 0, 0, axis_index_groups=rows_of, tiled=True))
    slab = jnp.stack(done, axis=2)
    return slab.transpose(1, 0, 2, 3).reshape(beams, cores * blocks * width)


def solution(mesh):
    placed = (P("grp", None, None, "sub"), P(), P(), P(), P(None, "grp", None, None, None))
    return jax.shard_map(
        body, mesh=mesh, in_specs=placed, out_specs=P("sub", "grp"), check_vma=False
    )
```

time: 610 us -> 179 us (0.29)
  waiting for transfers between devices: 310 us -> 65.3 us
  local copies, waits for them, and re-layouts: 134 us -> 8.39 us
  matrix products: 113 us -> 0 us
  Pallas kernels: 0 us -> 43.6 us
  blocking collectives: 0 us -> 31.6 us
  other arithmetic: 17.9 us -> 0.07 us
    all_to_all x1 -> x3, waiting for transfers between devices: 202 us -> 13.5 us  [the longest x1 8.05 us: body(): lax.all_to_all(by_owner, 'sub', 0, 0, axis_index_groups=rows_of, tiled=True)]
    dot_general x7 -> x0, matrix products: 113 us -> none  [the longest x3 53.6 us: body(): jnp.einsum('sbk,bkj->sbj', current.reshape(beam_count, block_count, block...]
    gather x7 -> x0, local copies, waits for them, and re-layouts: 98.4 us -> none  [the longest x3 43.9 us: body(): self_mats = jnp.take(bank, index_table[section_level, :, 0], axis=0)]
    ppermute x3 -> x0, waiting for transfers between devices: 46.5 us -> none  [from_partner(): return lax.ppermute(value, axis, pairs)]
    pallas_call x0 -> x1, Pallas kernels: none -> 43.6 us  [images_of(): pl.pallas_call(functools.partial(merge_tree, levels, blocks), grid_spec=p...]
    all_to_all x0 -> x3, blocking collectives: none -> 31.6 us  [the longest x1 11.3 us: body(): lax.all_to_all(by_owner, 'sub', 0, 0, axis_index_groups=rows_of, tiled=True)]
    all_to_all x1 -> x0, local copies, waits for them, and re-layouts: 22.5 us -> none  [body(): lax.all_to_all(pulse_rows, 'sub', split_axis=0, concat_axis=2, tiled=True)]
    select_n x2 -> x0, other arithmetic: 14.2 us -> none  [body(): picked = jnp.take(held_pulses, footprint.reshape(-1), axis=0)]
  transfers between devices with their start and end apart: 5 -> 5, of which waited for: 4 -> 4; matrix products, arithmetic and copies ran while one was open for 23% -> 0% of each run, Pallas kernels for 0% -> 0%
where the time goes in v1:
time: 179 us
  waiting for transfers between devices  65.3 us (36%)
  Pallas kernels  43.6 us (24%)
  blocking collectives  31.6 us (18%)
  starting transfers between devices  16.5 us (9%)
  between operations  13.5 us (8%)
  local copies, waits for them, and re-layouts  8.39 us (5%)
    reduce_scatter x2, waiting for transfers between devices, body(): summed = lax.psum_scatter(part, 'grp', scatter_dimension=0, tiled=True)  51.1 us
    pallas_call x1, Pallas kernels, images_of(): pl.pallas_call(functools.partial(merge_tree, levels, blocks), grid_spec=p...  43.6 us
    all_to_all x1, blocking collectives, body(): lax.all_to_all(by_owner, 'sub', 0, 0, axis_index_groups=rows_of, tiled=True)  11.3 us
    all_to_all x1, blocking collectives, body(): lax.all_to_all(summed[0], 'sub', 0, 0, axis_index_groups=lines_of, tiled=...  10.5 us
    all_to_all x1, blocking collectives, body(): turned = lax.all_to_all(spread, 'grp', 0, 0, tiled=True)  9.85 us
    all_to_all x1, starting transfers between devices, body(): lax.all_to_all(by_owner, 'sub', 0, 0, axis_index_groups=rows_of, tiled=True)  8.92 us
    all_to_all x1, waiting for transfers between devices, body(): lax.all_to_all(by_owner, 'sub', 0, 0, axis_index_groups=rows_of, tiled=True)  8.05 us
    all_to_all x1, waiting for transfers between devices, body(): turned = lax.all_to_all(spread, 'grp', 0, 0, tiled=True)  5.42 us
  transfers between devices with their start and end apart: 5, of which 4 were waited for; matrix products, arithmetic and copies ran while one was open for 0% of the time, Pallas kernels for 0%

profile of v1, /device:TPU:1, one launch (start us, length us, event | category | flops | bytes accessed | tf_op | source)
XLA Modules:
  0.0 178.9 jit_solution(10395528959123182350)
XLA Ops:
  6.5 0.1 reshape.26.pick_ref
  6.6 0.8 copy.11
  7.4 0.1 reshape.27.foot_ref
  7.5 0.2 constant_dynamic-slice_fusion
  7.7 0.7 copy.12
  8.4 0.2 reshape.28.table_ref
  8.6 2.2 %copy-done.1 = bf16[8,512,512]{2,1,0:T(8,128)(2,1)S(1)} copy-done((bf16[8,512,512]{2,1,0:T(8,128)(2,1)S(1)}, bf16[8,512,512]{2,1,0:T(8,128)(2,1)}, u32[]{:S(2)}) %copy-start.1) | copy-done | bytes 4194328
  10.7 1.1 copy-done.2
  11.9 43.6 %shard_map.55 = (bf16[4,4,96,512]{3,2,1,0:T(8,128)(2,1)}, bf16[4,4,96,512]{3,2,1,0:T(8,128)(2,1)}) custom-call(s32[8]{0:T(128)S(1)} %reshape.26.pick_ref, s32[64]{0:T(128)S(1)} %reshape.27.foot_ref, s32[384]{0:T(512)S(1)} %reshape.28.table_ref, bf16[32,128,1024]{2,1,0:T(8,128)(2,1)} %bitcast.24, bf16[32,48,256]{2,1,0:T(8,128)(2,1)S(1)} %copy-done.2, ...), custom_call_target="tpu_custom_call" | custom-call | flops 11200000000 | bytes 29360128 | tf_op jit(solution)/shard_map/pallas_call | solution.py:80
  55.5 0.7 reduce-scatter.3.cloned.1.call-update
  56.2 27.4 %reduce-scatter.5.cloned.1.call-done = bf16[1,4,96,512]{3,2,1,0:T(8,128)(2,1)} async-done(((bf16[4,4,96,512]{3,2,1,0:T(8,128)(2,1)}), bf16[1,4,96,512]{3,2,1,0:T(8,128)(2,1)}) %reduce-scatter.5.cloned.1.call-update) | async-done | bytes 393232 | tf_op jit(solution)/shard_map/reduce_scatter | solution.py:117
  83.6 4.0 %all-to-all-start.3 = ((bf16[4,96,512]{2,1,0:T(8,128)(2,1)}), bf16[4,96,512]{2,1,0:T(8,128)(2,1)S(1)}, u32[]{:S(2)}, u32[]{:S(2)}) async-start(bf16[4,96,512]{2,1,0:T(8,128)(2,1)} %bitcast.22), calls=%async_computation.5 | async-start | bytes 786432 | tf_op jit(solution)/shard_map/all_to_all | solution.py:118
  87.7 23.7 %reduce-scatter.3.cloned.1.call-done = bf16[1,4,96,512]{3,2,1,0:T(8,128)(2,1)} async-done(((bf16[4,4,96,512]{3,2,1,0:T(8,128)(2,1)}), bf16[1,4,96,512]{3,2,1,0:T(8,128)(2,1)}) %reduce-scatter.3.cloned.1.call-update) | async-done | bytes 393232 | tf_op jit(solution)/shard_map/reduce_scatter | solution.py:117
  111.4 10.5 %all_to_all.30 = bf16[4,96,512]{2,1,0:T(8,128)(2,1)} all-to-all(bf16[4,96,512]{2,1,0:T(8,128)(2,1)} %bitcast.23), channel_id=1, replica_groups={{0,8,16,24},{1,9,17,25},{2,10,18,26},{3,11,19,27},{4,12,20,28},{5,13,21..., dimensions={0} | all-to-all | bytes 786432 | tf_op jit(solution)/shard_map/all_to_all | solution.py:118
  121.9 9.8 %all_to_all.31 = bf16[4,96,512]{2,1,0:T(8,128)(2,1)S(1)} all-to-all(bf16[4,96,512]{2,1,0:T(8,128)(2,1)S(1)} %all-to-all-done.3), channel_id=1, replica_groups=mesh['grp'=4,'sub'=32] {'grp'}, dimensions={0} | all-to-all | bytes 786432 | tf_op jit(solution)/shard_map/all_to_all | solution.py:119
  131.7 3.5 %all-to-all-start.1 = ((bf16[4,96,512]{2,1,0:T(8,128)(2,1)}), bf16[4,96,512]{2,1,0:T(8,128)(2,1)S(1)}, u32[]{:S(2)}, u32[]{:S(2)}) async-start(bf16[4,96,512]{2,1,0:T(8,128)(2,1)} %all_to_all.30), calls=%async_computation.2 | async-start | bytes 786432 | tf_op jit(solution)/shard_map/all_to_all | solution.py:119
  135.2 0.8 copy.14
  136.0 5.4 %all-to-all-done.1 = bf16[4,96,512]{2,1,0:T(8,128)(2,1)S(1)} async-done(((bf16[4,96,512]{2,1,0:T(8,128)(2,1)}), bf16[4,96,512]{2,1,0:T(8,128)(2,1)S(1)}, u32[]{:S(2)}, u32[]{:S(2)}) %all-to-all-start.1) | async-done | bytes 393248 | tf_op jit(solution)/shard_map/all_to_all | solution.py:119
  141.4 8.9 %all-to-all-start.5 = ((bf16[8,48,512]{2,1,0:T(8,128)(2,1)}), bf16[8,48,512]{2,1,0:T(8,128)(2,1)S(1)}, u32[]{:S(2)}, u32[]{:S(2)}) async-start(bf16[8,48,512]{2,1,0:T(8,128)(2,1)} %bitcast.9), calls=%async_computation.7 | async-start | bytes 786432 | tf_op jit(solution)/shard_map/all_to_all | solution.py:121
  150.3 8.0 %all-to-all-done.5 = bf16[8,48,512]{2,1,0:T(8,128)(2,1)S(1)} async-done(((bf16[8,48,512]{2,1,0:T(8,128)(2,1)}), bf16[8,48,512]{2,1,0:T(8,128)(2,1)S(1)}, u32[]{:S(2)}, u32[]{:S(2)}) %all-to-all-start.5) | async-done | bytes 393248 | tf_op jit(solution)/shard_map/all_to_all | solution.py:121
  158.4 11.3 %all_to_all.32 = bf16[8,48,512]{2,1,0:T(8,128)(2,1)S(1)} all-to-all(bf16[8,48,512]{2,1,0:T(8,128)(2,1)S(1)} %bitcast.19), channel_id=1, replica_groups={{0,1,2,3,4,5,6,7},{8,9,10,11,12,13,14,15},{16,17,18,19,20,21,22,23},{24..., dimensions={0} | all-to-all | bytes 786432 | tf_op jit(solution)/shard_map/all_to_all | solution.py:121
  169.7 0.1 maximum_bitcast_fusion
  169.8 0.8 copy.15
  170.6 1.5 reshape.33
  (10 shorter events, 0.1 us)
Async XLA Ops:
  6.5 1.0 copy-start
  6.5 77.1 %reduce-scatter.5.cloned.1.call-start = ((), (), s32[]{:S(2)}) async-start(), calls=%async_computation.9 | async-start | bytes 1966080 | tf_op jit(solution)/shard_map/reduce_scatter | solution.py:117
  8.5 2.2 %copy-start.1 = (bf16[8,512,512]{2,1,0:T(8,128)(2,1)S(1)}, bf16[8,512,512]{2,1,0:T(8,128)(2,1)}, u32[]{:S(2)}) copy-start(bf16[8,512,512]{2,1,0:T(8,128)(2,1)} %bank_ref.1) | copy-start | bytes 12582916
  10.7 1.1 copy-start.2
  55.5 55.9 %reduce-scatter.3.cloned.1.call-start = ((), (), s32[]{:S(2)}) async-start(), calls=%async_computation.8 | async-start | bytes 1966080 | tf_op jit(solution)/shard_map/reduce_scatter | solution.py:117
  83.6 27.8 %all-to-all-start.3 = ((bf16[4,96,512]{2,1,0:T(8,128)(2,1)}), bf16[4,96,512]{2,1,0:T(8,128)(2,1)S(1)}, u32[]{:S(2)}, u32[]{:S(2)}) async-start(bf16[4,96,512]{2,1,0:T(8,128)(2,1)} %bitcast.22), calls=%async_computation.5 | async-start | bytes 786432 | tf_op jit(solution)/shard_map/all_to_all | solution.py:118
  131.7 9.7 %all-to-all-start.1 = ((bf16[4,96,512]{2,1,0:T(8,128)(2,1)}), bf16[4,96,512]{2,1,0:T(8,128)(2,1)S(1)}, u32[]{:S(2)}, u32[]{:S(2)}) async-start(bf16[4,96,512]{2,1,0:T(8,128)(2,1)} %all_to_all.30), calls=%async_computation.2 | async-start | bytes 786432 | tf_op jit(solution)/shard_map/all_to_all | solution.py:119
  141.4 17.0 %all-to-all-start.5 = ((bf16[8,48,512]{2,1,0:T(8,128)(2,1)}), bf16[8,48,512]{2,1,0:T(8,128)(2,1)S(1)}, u32[]{:S(2)}, u32[]{:S(2)}) async-start(bf16[8,48,512]{2,1,0:T(8,128)(2,1)} %bitcast.9), calls=%async_computation.7 | async-start | bytes 786432 | tf_op jit(solution)/shard_map/all_to_all | solution.py:121
Sparse Core Ops, SparseCore 0:
  55.6 27.9 reduce-scatter.4
  86.1 25.3 reduce-scatter.2

commit v2 on v0

v2 whole, which is shorter than its diff:
```python
import functools
import jax
import jax.numpy as jnp
from jax import lax
from jax.experimental import pallas as pl
from jax.experimental.pallas import tpu as pltpu
from jax.sharding import PartitionSpec as P

CHUNK = 4
ROUND = 12
LINE, CORES, TEAM, RING = 4, 2, 8, 4
VMEM = 56 * 2**20

f32, bf16, i32 = jnp.float32, jnp.bfloat16, jnp.int32
ANY = pl.BlockSpec(memory_space=pl.ANY)


def where_am_i():
    sub = lax.axis_index("sub")
    return lax.axis_index("grp"), sub >> 3, (sub >> 1) & 3, sub & 1


def run(copies):
    for c in copies:
        c.start()
    for c in copies:
        c.wait()


def row_fetches(block, pulses_ref, rows, row_sem):
    width = rows.shape[2]
    return [
        pltpu.make_async_copy(pulses_ref.at[j, :, pl.ds(block * width, width)], rows.at[j], row_sem.at[j])
        for j in range(rows.shape[0])
    ]


def project(foot, weights, rows, image):
    for o in range(weights.shape[0]):
        both = jnp.concatenate([rows[o], rows[foot[1, o]]], axis=0)
        image[o] = jnp.dot(weights[o], both, preferred_element_type=f32).astype(bf16)


def start_kernel(block, foot_ref, pulses_ref, weight_ref, *rest):
    outs, (foot, rows, weights, image, row_sem, sem, out_sem) = rest[:RING], rest[RING:]
    first = [pltpu.make_async_copy(foot_ref, foot, sem.at[0]), pltpu.make_async_copy(weight_ref, weights, sem.at[1])]
    copies = first + row_fetches(block, pulses_ref, rows, row_sem)
    run(copies)
    project(foot, weights, rows, image)
    _, z, _, _ = where_am_i()
    run([
        pltpu.make_async_copy(image.at[pl.ds(((z + d) & 3) * TEAM, TEAM)], outs[d], out_sem.at[d])
        for d in (1, 3, 2, 0)
    ])


def start_images(block, foot, pulses, weight, width):
    owners, beams, depth = weight.shape
    return pl.pallas_call(
        functools.partial(start_kernel, block),
        in_specs=[ANY] * 3,
        out_specs=[ANY] * RING,
        out_shape=[jax.ShapeDtypeStruct((TEAM, beams, width), bf16)] * RING,
        scratch_shapes=[
            pltpu.SMEM(foot.shape, i32),
            pltpu.VMEM((owners, depth // 2, width), bf16),
            pltpu.VMEM((owners, beams, depth), bf16),
            pltpu.VMEM((owners, beams, width), bf16),
            pltpu.SemaphoreType.DMA((owners,)),
            pltpu.SemaphoreType.DMA((2,)),
            pltpu.SemaphoreType.DMA((RING,)),
        ],
        compiler_params=pltpu.CompilerParams(vmem_limit_bytes=VMEM),
        cost_estimate=pl.CostEstimate(flops=400_000_000, bytes_accessed=7 * 2**20, transcendentals=0),
        name="start",
    )(foot, pulses, weight)


def tree_kernel(joined, block, levels, *refs):
    if joined:
        part_refs, (index_ref, bank_ref), refs = refs[:RING], refs[RING:RING + 2], refs[RING + 2:]
        outs, refs = refs[:5], refs[5:]
    else:
        (foot_ref, pulses_ref, weight_ref, _, index_ref, bank_ref), refs = refs[:6], refs[6:]
        outs, refs = refs[:RING], refs[RING:]
    index, mats, image, acc, stage, sem, row_sem, mat_sem, out_sem = refs[:9]
    lists, refs = refs[9:9 + 5 * 2 * levels], refs[9 + 5 * 2 * levels:]
    images, beams, width = stage.shape[0] - 1, stage.shape[1], stage.shape[2]
    kinds = mats.shape[0]
    passes = 2 * levels
    most = (images + kinds * (CHUNK - 1)) // CHUNK
    y, z, x, c = where_am_i()
    blocks = index.shape[3] // (RING * TEAM)

    index_copy = pltpu.make_async_copy(index_ref, index, sem.at[0])
    mat_copies = [pltpu.make_async_copy(bank_ref.at[k], mats.at[k], mat_sem.at[k]) for k in range(kinds)]
    if joined:
        feeds = [
            pltpu.make_async_copy(part_refs[d], image.at[0, pl.ds(d * TEAM, TEAM)], row_sem.at[d])
            for d in range(RING)
        ]
    else:
        foot, rows, weights = refs
        feeds = [
            pltpu.make_async_copy(foot_ref, foot, sem.at[1]),
            pltpu.make_async_copy(weight_ref, weights, sem.at[2]),
        ] + row_fetches(block, pulses_ref, rows, row_sem)
    for copy in [index_copy] + feeds + mat_copies:
        copy.start()

    def kind_of(p, i):
        if joined:
            owner = z * TEAM + i % TEAM
            column = (((z - i // TEAM) & 3) * TEAM + x * CORES + c) * blocks + block
        else:
            owner = i
            column = ((z * LINE + x) * CORES + c) * blocks + block
        return index[p // 2, owner, p % 2, column]

    def sort_pass(p):
        counts, starts, ranks, slots, entries = lists[5 * p:5 * p + 5]
        for k in range(kinds):
            counts[k] = 0
        for q in range(most):
            entries[q] = 0
            for i in range(CHUNK):
                slots[q * CHUNK + i] = images
        for i in range(images):
            k = kind_of(p, i)
            n = counts[k]
            ranks[i] = n
            counts[k] = n + 1
        begin = 0
        for k in range(kinds):
            starts[k] = begin * CHUNK
            begin = begin + ((counts[k] + (CHUNK - 1)) >> 2)
        for i in range(images):
            k = kind_of(p, i)
            place = starts[k] + ranks[i]
            slots[place] = i
            entries[place >> 2] = k
        return begin

    def chunk(p, q):
        level, which = p // 2, p % 2
        slots, entries = lists[5 * p + 3:5 * p + 5]
        now, later = level % 2, (level + 1) % 2
        dest = [slots[q * CHUNK + i] for i in range(CHUNK)]
        source = [d if which == 0 else jnp.bitwise_xor(d, 1 << level) for d in dest]
        many = jnp.concatenate([image[now, s] for s in source], axis=0)
        out = jnp.dot(many, mats[entries[q]], preferred_element_type=f32)
        for i, d in enumerate(dest):
            part = out[i * beams:(i + 1) * beams]
            if which == 0:
                acc[d] = part
            elif level + 1 < levels:
                image[later, d] = (acc[d] + part).astype(bf16)
            else:
                xo, co = (d >> 1) & 3, d & 1
                if joined:
                    place = ((((z - (d >> 3)) & 3) - y) & 3) * TEAM + ((xo - x) & 3) * CORES + co
                else:
                    place = ((xo - y) & 3) * TEAM + (((d >> 3) - z) & 3) * CORES + co
                stage[jnp.where(d == images, images, place)] = (acc[d] + part).astype(bf16)

    index_copy.wait()
    used = sort_pass(0)
    for copy in feeds:
        copy.wait()
    if not joined:
        project(foot, weights, rows, image.at[0])
    for copy in mat_copies:
        copy.wait()
    for p in range(passes):
        after = sort_pass(p + 1) if p + 1 < passes else None
        for q in range(ROUND):
            chunk(p, q)

        @pl.when(used > ROUND)
        def _(p=p):
            for q in range(ROUND, most):
                chunk(p, q)

        used = after

    half = TEAM // 2
    if joined:
        moves = [
            (2 * TEAM, half, outs[0].at[0]), (TEAM + half, half, outs[0].at[1]),
            (2 * TEAM + half, half, outs[1].at[0]), (3 * TEAM, half, outs[1].at[1]),
            (TEAM, half, outs[2]), (3 * TEAM + half, half, outs[3]), (0, TEAM, outs[4]),
        ]
    else:
        moves = [(r * TEAM, TEAM, outs[r]) for r in (2, 1, 3, 0)]
    run([
        pltpu.make_async_copy(stage.at[pl.ds(s, n)], ref, out_sem.at[i]) for i, (s, n, ref) in enumerate(moves)
    ])


def trees(joined, block, index, bank, beams, feeds):
    kinds, width, _ = bank.shape
    levels, images = index.shape[:2]
    most = (images + kinds * (CHUNK - 1)) // CHUNK
    whole = jax.ShapeDtypeStruct((TEAM, beams, width), bf16)
    pair = jax.ShapeDtypeStruct((2, TEAM // 2, beams, width), bf16)
    piece = jax.ShapeDtypeStruct((TEAM // 2, beams, width), bf16)
    scratch = [
        pltpu.SMEM(index.shape, i32),
        pltpu.VMEM(bank.shape, bf16),
        pltpu.VMEM((2, images + TEAM, beams, width), bf16),
        pltpu.VMEM((images + 1, beams, width), f32),
        pltpu.VMEM((images + 1, beams, width), bf16),
        pltpu.SemaphoreType.DMA((3,)),
        pltpu.SemaphoreType.DMA((images,)),
        pltpu.SemaphoreType.DMA((kinds,)),
        pltpu.SemaphoreType.DMA((7,)),
    ]
    for _ in range(2 * levels):
        scratch += [pltpu.SMEM((n,), i32) for n in (kinds, kinds, images, most * CHUNK, most)]
    if not joined:
        foot, pulses, weight, _ = feeds
        owners, _, depth = weight.shape
        scratch += [
            pltpu.SMEM(foot.shape, i32),
            pltpu.VMEM((owners, depth // 2, width), bf16),
            pltpu.VMEM((owners, beams, depth), bf16),
        ]
    out_shape = [pair, pair, piece, piece, whole] if joined else [whole] * RING
    return pl.pallas_call(
        functools.partial(tree_kernel, joined, block, levels),
        in_specs=[ANY] * (len(feeds) + 2),
        out_specs=[ANY] * len(out_shape),
        out_shape=out_shape,
        scratch_shapes=scratch,
        compiler_params=pltpu.CompilerParams(vmem_limit_bytes=VMEM),
        cost_estimate=pl.CostEstimate(flops=9_000_000_000, bytes_accessed=11 * 2**20, transcendentals=0),
        name="joined_trees" if joined else "trees",
    )(*feeds, index, bank)


def lay_kernel(*refs):
    mine, other, out_ref = refs[:-2], refs[-2], refs[-1]
    _, _, x, c = where_am_i()
    width = other.shape[2]
    blocks = len(mine) // LINE
    for b in range(blocks):
        for d in range(LINE):
            for part, core in ((mine[b * LINE + d][c], c), (other[b * LINE + d], 1 - c)):
                at = ((((x - d) & 3) * CORES + core) * blocks + b) * width
                out_ref[:, pl.ds(pl.multiple_of(at, width), width)] = part


def total(*parts):
    out = parts[0].astype(f32)
    for part in parts[1:]:
        out = out + part.astype(f32)
    return out.astype(bf16)


def turn(pieces, shift):
    return [lax.select_n((shift - d) & 3, *pieces) for d in range(len(pieces))]


def body(pulses, footprint, proj_weight, bank, merge_index):
    held = pulses[0]
    width = bank.shape[1]
    owners, beams, _ = proj_weight.shape
    y, z, x, c = where_am_i()
    foot = footprint.T
    index = merge_index[:, 0].transpose(0, 1, 3, 2)

    def along_y(value, d):
        return lax.ppermute(value, "grp", [(i, (i + d) % RING) for i in range(RING)])

    def along_sub(value, move):
        return lax.ppermute(value, "sub", [(i, move(i >> 3, (i >> 1) & 3, i & 1)) for i in range(owners)])

    def along_z(value, d):
        return along_sub(value, lambda zz, xx, cc: ((zz + d) % RING) * TEAM + xx * CORES + cc)

    def along_x(value, d):
        return along_sub(value, lambda zz, xx, cc: zz * TEAM + ((xx + d) % LINE) * CORES + cc)

    def exchange(pieces, along):
        return [pieces[0]] + [along(pieces[d], d) for d in range(1, len(pieces))]

    begun = start_images(0, foot, held, proj_weight, width)
    spread = exchange(begun, along_z)
    sent = trees(False, 1, index, bank, beams, (foot, held, proj_weight, begun[0]))
    got = exchange(sent, along_y)
    to_up, to_down, keep_up, keep_down, own = trees(True, 0, index, bank, beams, tuple(spread))
    got, own = lax.optimization_barrier((got, own))
    from_down, from_up = along_y(to_up, 1), along_y(to_down, -1)
    last_down = along_y(total(from_down[0], keep_up), 1)
    last_up = along_y(total(from_up[0], keep_down), -1)
    half = TEAM // 2

    summed = []
    for r in range(LINE):
        low = r * CORES < half
        lo = r * CORES - (0 if low else half)
        near, far = (last_down, from_up[1]) if low else (last_up, from_down[1])
        summed.append(total(own[r * CORES:(r + 1) * CORES], near[lo:lo + CORES], far[lo:lo + CORES]))
    first = exchange(summed, along_x)

    pieces = [total(*[g[r * CORES:(r + 1) * CORES] for g in got]) for r in range(RING)]
    pieces = exchange(pieces, along_z)
    pieces = exchange(turn(pieces, z - y), along_y)
    second = exchange(turn(pieces, y - x), along_x)
    mine = first + second
    other = jnp.stack([jnp.where(c == 0, piece[1], piece[0]) for piece in mine])
    other = along_sub(other, lambda zz, xx, cc: zz * TEAM + xx * CORES + 1 - cc)

    return pl.pallas_call(
        lay_kernel,
        out_shape=jax.ShapeDtypeStruct((beams, LINE * CORES * 2 * width), bf16),
        name="lay",
    )(*mine, other)


def solution(mesh):
    placed = (P("grp", None, None, "sub"), P(), P(), P(), P(None, "grp", None, None, None))
    return jax.shard_map(
        body, mesh=mesh, in_specs=placed, out_specs=P("sub", "grp"), check_vma=False
    )
```

time: 610 us -> 106 us (0.17)
  waiting for transfers between devices: 310 us -> 21.2 us
  local copies, waits for them, and re-layouts: 134 us -> 2.25 us
  matrix products: 113 us -> 0 us
  Pallas kernels: 0 us -> 43.8 us
  other arithmetic: 17.9 us -> 3.63 us
  starting transfers between devices: 21.1 us -> 34.9 us
  between operations: 13.5 us -> 0.33 us
    all_to_all x1 -> x0, waiting for transfers between devices: 202 us -> none  [body(): lax.all_to_all(pulse_rows, 'sub', split_axis=0, concat_axis=2, tiled=True)]
    dot_general x7 -> x0, matrix products: 113 us -> none  [the longest x3 53.6 us: body(): jnp.einsum('sbk,bkj->sbj', current.reshape(beam_count, block_count, block...]
    gather x7 -> x0, local copies, waits for them, and re-layouts: 98.4 us -> none  [the longest x3 43.9 us: body(): self_mats = jnp.take(bank, index_table[section_level, :, 0], axis=0)]
    reduce_scatter x1 -> x0, waiting for transfers between devices: 62.1 us -> none  [body(): summed = lax.psum_scatter(current, 'grp', scatter_dimension=1, tiled=True)]
    pallas_call x0 -> x4, Pallas kernels: none -> 43.8 us  [the longest x2 36 us: trees(): pl.pallas_call(functools.partial(tree_kernel, joined, block, levels), in_...]
    ppermute x3 -> x23, waiting for transfers between devices: 46.5 us -> 21.2 us  [the longest x13 14.3 us: along_sub(): lax.ppermute(value, 'sub', [(i, move(i >> 3, i >> 1 & 3, i & 1)) for i in...]
    ppermute x3 -> x23, starting transfers between devices: 11.6 us -> 34.9 us  [the longest x13 21.5 us: along_sub(): lax.ppermute(value, 'sub', [(i, move(i >> 3, i >> 1 & 3, i & 1)) for i in...]
    all_to_all x1 -> x0, local copies, waits for them, and re-layouts: 22.5 us -> none  [body(): lax.all_to_all(pulse_rows, 'sub', split_axis=0, concat_axis=2, tiled=True)]
  transfers between devices with their start and end apart: 5 -> 23, of which waited for: 4 -> 9; matrix products, arithmetic and copies ran while one was open for 23% -> 3% of each run, Pallas kernels for 0% -> 34%
where the time goes in v2:
time: 106 us
  Pallas kernels  43.8 us (41%)
  starting transfers between devices  34.9 us (33%)
  waiting for transfers between devices  21.2 us (20%)
  other arithmetic  3.63 us (3%)
  local copies, waits for them, and re-layouts  2.25 us (2%)
    pallas_call x2, Pallas kernels, trees(): pl.pallas_call(functools.partial(tree_kernel, joined, block, levels), in_...  36 us
    ppermute x13, starting transfers between devices, along_sub(): lax.ppermute(value, 'sub', [(i, move(i >> 3, i >> 1 & 3, i & 1)) for i in...  21.5 us
    ppermute x13, waiting for transfers between devices, along_sub(): lax.ppermute(value, 'sub', [(i, move(i >> 3, i >> 1 & 3, i & 1)) for i in...  14.3 us
    ppermute x10, starting transfers between devices, along_y(): lax.ppermute(value, 'grp', [(i, (i + d) % RING) for i in range(RING)])  13.4 us
    ppermute x10, waiting for transfers between devices, along_y(): lax.ppermute(value, 'grp', [(i, (i + d) % RING) for i in range(RING)])  6.84 us
    pallas_call x1, Pallas kernels, start_images(): pl.pallas_call(functools.partial(start_kernel, block), in_specs=[ANY] * 3...  5.54 us
    convert_element_type x4, other arithmetic, total(): return out.astype(bf16)  3.3 us
    pallas_call x1, Pallas kernels, body(): pl.pallas_call(lay_kernel, out_shape=jax.ShapeDtypeStruct((beams, LINE *...  2.28 us
  transfers between devices with their start and end apart: 23, of which 9 were waited for; matrix products, arithmetic and copies ran while one was open for 3% of the time, Pallas kernels for 34%

profile of v2, /device:TPU:1, one launch (start us, length us, event | category | flops | bytes accessed | tf_op | source)
XLA Modules:
  0.0 106.0 jit_solution(2172042848427676445)
XLA Ops:
  0.0 5.5 %start.1 = (bf16[8,48,512]{2,1,0:T(8,128)(2,1)}, bf16[8,48,512]{2,1,0:T(8,128)(2,1)}, bf16[8,48,512]{2,1,0:T(8,128)(2,1)}, bf16[8,48,512]{2,1,0:T(8,128)(2,1)}) custom-call(s32[2,32]{1,0:T(2,128)} %bitcast.37, bf16[32,128,1024]{2,1,0:T(8,128)(2,1)} %bitcast.35, bf16[32,48,256]{2,1,0:T(8,128)(2,1)} %refs_2_.1), custom_call_target="tpu_custom_call" | custom-call | flops 400000000 | bytes 7340032 | tf_op jit(solution)/shard_map/start/pallas_call | solution.py:59
  5.5 2.5 %collective-permute-start.3 = (bf16[8,48,512]{2,1,0:T(8,128)(2,1)}, bf16[8,48,512]{2,1,0:T(8,128)(2,1)S(1)}, u32[]{:S(2)}, u32[]{:S(2)}) collective-permute-start(bf16[8,48,512]{2,1,0:T(8,128)(2,1)} %get-tuple-element.28), channel_id=1, source_target_pairs={{0,8},{1,9},{2,10},{3,11},{4,12},{5,13},{6,14},{7,15},{8,16},{9,17... | collective-permute-start | bytes 1179656 | tf_op jit(solution)/shard_map/ppermute | solution.py:276
  8.1 3.3 %collective-permute-start.4 = (bf16[8,48,512]{2,1,0:T(8,128)(2,1)}, bf16[8,48,512]{2,1,0:T(8,128)(2,1)S(1)}, u32[]{:S(2)}, u32[]{:S(2)}) collective-permute-start(bf16[8,48,512]{2,1,0:T(8,128)(2,1)} %get-tuple-element.29), channel_id=1, source_target_pairs={{0,16},{1,17},{2,18},{3,19},{4,20},{5,21},{6,22},{7,23},{8,24},{9,... | collective-permute-start | bytes 1179656 | tf_op jit(solution)/shard_map/ppermute | solution.py:276
  12.1 19.0 %trees.1 = (bf16[8,48,512]{2,1,0:T(8,128)(2,1)}, bf16[8,48,512]{2,1,0:T(8,128)(2,1)}, bf16[8,48,512]{2,1,0:T(8,128)(2,1)}, bf16[8,48,512]{2,1,0:T(8,128)(2,1)}) custom-call(s32[2,32]{1,0:T(2,128)} %bitcast.38, bf16[32,128,1024]{2,1,0:T(8,128)(2,1)} %bitcast.36, bf16[32,48,256]{2,1,0:T(8,128)(2,1)} %refs_2_.1, ...), custom_call_target="tpu_custom_call" | custom-call | flops 8999999488 | bytes 11534336 | tf_op jit(solution)/shard_map/trees/pallas_call | solution.py:229
  31.1 1.4 %collective-permute-start = (bf16[8,48,512]{2,1,0:T(8,128)(2,1)}, bf16[8,48,512]{2,1,0:T(8,128)(2,1)S(1)}, u32[]{:S(2)}, u32[]{:S(2)}) collective-permute-start(bf16[8,48,512]{2,1,0:T(8,128)(2,1)} %get-tuple-element.25), channel_id=1, source_target_pairs={{0,32},{32,64},{64,96},{96,0},{1,33},{33,65},{65,97},{97,1},{2,34}... | collective-permute-start | bytes 1179656 | tf_op jit(solution)/shard_map/ppermute | solution.py:273
  32.5 2.6 %collective-permute-start.1 = (bf16[8,48,512]{2,1,0:T(8,128)(2,1)}, bf16[8,48,512]{2,1,0:T(8,128)(2,1)S(1)}, u32[]{:S(2)}, u32[]{:S(2)}) collective-permute-start(bf16[8,48,512]{2,1,0:T(8,128)(2,1)} %get-tuple-element.26), channel_id=1, source_target_pairs={{0,64},{32,96},{64,0},{96,32},{1,65},{33,97},{65,1},{97,33},{2,66}... | collective-permute-start | bytes 1179656 | tf_op jit(solution)/shard_map/ppermute | solution.py:273
  37.7 17.0 %joined_trees.1 = (bf16[2,4,48,512]{3,2,1,0:T(8,128)(2,1)}, bf16[2,4,48,512]{3,2,1,0:T(8,128)(2,1)}, bf16[4,48,512]{2,1,0:T(8,128)(2,1)}, bf16[4,48,512]{2,1,0:T(8,128)(2,1)}, bf16[8,48,512]{2,1,0:T(8,128)(2,1)}) custom-call(bf16[8,48,512]{2,1,0:T(8,128)(2,1)} %get-tuple-element.23.refs_3_.refs_0_, bf16[8,48,512]{2,1,0:T(8,128)(2,1)} %copy-done.10, ...), custom_call_target="tpu_custom_call" | custom-call | flops 8999999488 | bytes 11534336 | tf_op jit(solution)/shard_map/joined_trees/pallas_call | solution.py:229
  55.7 2.0 %collective-permute-start.15 = (bf16[2,48,512]{2,1,0:T(8,128)(2,1)S(1)}, bf16[2,48,512]{2,1,0:T(8,128)(2,1)S(1)}, u32[]{:S(2)}, u32[]{:S(2)}) collective-permute-start(bf16[2,48,512]{2,1,0:T(8,128)(2,1)S(1)} %get-tuple-element.46), channel_id=1, source_target_pairs={{0,24},{1,25},{2,26},{3,27},{4,28},{5,29},{6,30},{7,31},{8,0},{9,1... | collective-permute-start | bytes 294920 | tf_op jit(solution)/shard_map/ppermute | solution.py:276
  58.5 1.5 %collective-permute-done.13 = bf16[2,48,512]{2,1,0:T(8,128)(2,1)S(1)} collective-permute-done((bf16[2,48,512]{2,1,0:T(8,128)(2,1)S(1)}, bf16[2,48,512]{2,1,0:T(8,128)(2,1)S(1)}, u32[]{:S(2)}, u32[]{:S(2)}) %collective-permute-start.13) | collective-permute-done | bytes 98336 | tf_op jit(solution)/shard_map/ppermute | solution.py:276
  60.0 1.3 %collective-permute-done.14 = bf16[2,48,512]{2,1,0:T(8,128)(2,1)S(1)} collective-permute-done((bf16[2,48,512]{2,1,0:T(8,128)(2,1)S(1)}, bf16[2,48,512]{2,1,0:T(8,128)(2,1)S(1)}, u32[]{:S(2)}, u32[]{:S(2)}) %collective-permute-start.14) | collective-permute-done | bytes 98336 | tf_op jit(solution)/shard_map/ppermute | solution.py:276
  61.8 2.6 %collective-permute-start.18 = (bf16[2,48,512]{2,1,0:T(8,128)(2,1)S(1)}, bf16[2,48,512]{2,1,0:T(8,128)(2,1)S(1)}, u32[]{:S(2)}, u32[]{:S(2)}) collective-permute-start(bf16[2,48,512]{2,1,0:T(8,128)(2,1)S(1)} %get-tuple-element.55), channel_id=1, source_target_pairs={{0,96},{32,0},{64,32},{96,64},{1,97},{33,1},{65,33},{97,65},{2,98}... | collective-permute-start | bytes 294920 | tf_op jit(solution)/shard_map/ppermute | solution.py:273
  64.4 2.7 %collective-permute-start.8 = (bf16[2,4,48,512]{3,2,1,0:T(8,128)(2,1)}, bf16[2,4,48,512]{3,2,1,0:T(8,128)(2,1)S(1)}, u32[]{:S(2)}, u32[]{:S(2)}) collective-permute-start(bf16[2,4,48,512]{3,2,1,0:T(8,128)(2,1)} %get-tuple-element.35), channel_id=1, source_target_pairs={{0,96},{32,0},{64,32},{96,64},{1,97},{33,1},{65,33},{97,65},{2,98}... | collective-permute-start | bytes 1179656 | tf_op jit(solution)/shard_map/ppermute | solution.py:273
  67.1 2.7 %collective-permute-done.17 = bf16[2,48,512]{2,1,0:T(8,128)(2,1)S(1)} collective-permute-done((bf16[2,48,512]{2,1,0:T(8,128)(2,1)S(1)}, bf16[2,48,512]{2,1,0:T(8,128)(2,1)S(1)}, u32[]{:S(2)}, u32[]{:S(2)}) %collective-permute-start.17) | collective-permute-done | bytes 98336 | tf_op jit(solution)/shard_map/ppermute | solution.py:273
  69.8 1.6 %collective-permute-done.16 = bf16[2,48,512]{2,1,0:T(8,128)(2,1)S(1)} collective-permute-done((bf16[2,48,512]{2,1,0:T(8,128)(2,1)S(1)}, bf16[2,48,512]{2,1,0:T(8,128)(2,1)S(1)}, u32[]{:S(2)}, u32[]{:S(2)}) %collective-permute-start.16) | collective-permute-done | bytes 98336 | tf_op jit(solution)/shard_map/ppermute | solution.py:273
  72.5 2.5 %collective-permute-done.8 = bf16[2,4,48,512]{3,2,1,0:T(8,128)(2,1)S(1)} collective-permute-done((bf16[2,4,48,512]{3,2,1,0:T(8,128)(2,1)}, bf16[2,4,48,512]{3,2,1,0:T(8,128)(2,1)S(1)}, u32[]{:S(2)}, u32[]{:S(2)}) %collective-permute-start.8) | collective-permute-done | bytes 393248 | tf_op jit(solution)/shard_map/ppermute | solution.py:273
  76.0 2.2 %collective-permute-start.10 = (bf16[4,48,512]{2,1,0:T(8,128)(2,1)S(1)}, bf16[4,48,512]{2,1,0:T(8,128)(2,1)S(1)}, u32[]{:S(2)}, u32[]{:S(2)}) collective-permute-start(bf16[4,48,512]{2,1,0:T(8,128)(2,1)S(1)} %fusion), channel_id=1, source_target_pairs={{0,96},{32,0},{64,32},{96,64},{1,97},{33,1},{65,33},{97,65},{2,98}... | collective-permute-start | bytes 589832 | tf_op jit(solution)/shard_map/ppermute | solution.py:273
  78.2 2.0 %collective-permute-start.19 = (bf16[2,48,512]{2,1,0:T(8,128)(2,1)S(1)}, bf16[2,48,512]{2,1,0:T(8,128)(2,1)S(1)}, u32[]{:S(2)}, u32[]{:S(2)}) collective-permute-start(bf16[2,48,512]{2,1,0:T(8,128)(2,1)S(1)} %get-tuple-element.53), channel_id=1, source_target_pairs={{0,2},{1,3},{2,4},{3,5},{4,6},{5,7},{6,0},{7,1},{8,10},{9,11},{10,... | collective-permute-start | bytes 294920 | tf_op jit(solution)/shard_map/ppermute | solution.py:276
  80.2 1.7 %collective-permute-start.20 = (bf16[2,48,512]{2,1,0:T(8,128)(2,1)S(1)}, bf16[2,48,512]{2,1,0:T(8,128)(2,1)S(1)}, u32[]{:S(2)}, u32[]{:S(2)}) collective-permute-start(bf16[2,48,512]{2,1,0:T(8,128)(2,1)S(1)} %get-tuple-element.52), channel_id=1, source_target_pairs={{0,4},{1,5},{2,6},{3,7},{4,0},{5,1},{6,2},{7,3},{8,12},{9,13},{10,... | collective-permute-start | bytes 294920 | tf_op jit(solution)/shard_map/ppermute | solution.py:276
  82.0 1.9 %collective-permute-start.21 = (bf16[2,48,512]{2,1,0:T(8,128)(2,1)S(1)}, bf16[2,48,512]{2,1,0:T(8,128)(2,1)S(1)}, u32[]{:S(2)}, u32[]{:S(2)}) collective-permute-start(bf16[2,48,512]{2,1,0:T(8,128)(2,1)S(1)} %get-tuple-element.41), channel_id=1, source_target_pairs={{0,6},{1,7},{2,0},{3,1},{4,2},{5,3},{6,4},{7,5},{8,14},{9,15},{10,... | collective-permute-start | bytes 294920 | tf_op jit(solution)/shard_map/ppermute | solution.py:276
  86.3 5.6 %collective-permute-done.9.refs_1_ = bf16[2,48,512]{2,1,0:T(8,128)(2,1)S(1)} collective-permute-done((bf16[2,48,512]{2,1,0:T(8,128)(2,1)S(1)}, bf16[2,48,512]{2,1,0:T(8,128)(2,1)S(1)}, u32[]{:S(2)}, u32[]{:S(2)}) %collective-permute-start.9) | collective-permute-done | bytes 98336 | tf_op jit(solution)/shard_map/ppermute | solution.py:276
  92.0 4.4 %collective-permute-done.12.refs_3_ = bf16[2,48,512]{2,1,0:T(8,128)(2,1)S(1)} collective-permute-done((bf16[2,48,512]{2,1,0:T(8,128)(2,1)S(1)}, bf16[2,48,512]{2,1,0:T(8,128)(2,1)S(1)}, u32[]{:S(2)}, u32[]{:S(2)}) %collective-permute-start.12) | collective-permute-done | bytes 98336 | tf_op jit(solution)/shard_map/ppermute | solution.py:276
  96.5 5.1 %collective-permute-start.22 = (bf16[8,48,512]{2,1,0:T(8,128)(2,1)S(1)}, bf16[8,48,512]{2,1,0:T(8,128)(2,1)S(1)}, u32[]{:S(2)}, u32[]{:S(2)}) collective-permute-start(bf16[8,48,512]{2,1,0:T(8,128)(2,1)S(1)} %fusion.6), channel_id=1, source_target_pairs={{0,1},{1,0},{2,3},{3,2},{4,5},{5,4},{6,7},{7,6},{8,9},{9,8},{10,11... | collective-permute-start | bytes 1179656 | tf_op jit(solution)/shard_map/ppermute | solution.py:276
  101.6 1.3 %collective-permute-done.22.refs_8_ = bf16[8,48,512]{2,1,0:T(8,128)(2,1)S(1)} collective-permute-done((bf16[8,48,512]{2,1,0:T(8,128)(2,1)S(1)}, bf16[8,48,512]{2,1,0:T(8,128)(2,1)S(1)}, u32[]{:S(2)}, u32[]{:S(2)}) %collective-permute-start.22) | collective-permute-done | bytes 393248 | tf_op jit(solution)/shard_map/ppermute | solution.py:276
  103.7 2.3 %lay.1 = bf16[48,8192]{1,0:T(8,128)(2,1)} custom-call(bf16[2,48,512]{2,1,0:T(8,128)(2,1)} %copy-done.1, bf16[2,48,512]{2,1,0:T(8,128)(2,1)} %copy-done.7, bf16[2,48,512]{2,1,0:T(8,128)(2,1)} %copy-done.8, bf16[2,48,512]{2,1,0:T(8,128)(2,1)} %copy-done.9, bf16[2,48,512]{2,1,0:T(8,128)(2,1)} %copy-done, bf16[2,48,512]{2,1,0:T(8,128)(2,1)} %copy-done.4, ...), custom_call_target="tpu_custom_call" | custom-call | tf_op jit(solution)/shard_map/lay/pallas_call | solution.py:314
  (68 shorter events, 11.0 us)
Async XLA Ops:
  5.5 29.6 %collective-permute-start.3 = (bf16[8,48,512]{2,1,0:T(8,128)(2,1)}, bf16[8,48,512]{2,1,0:T(8,128)(2,1)S(1)}, u32[]{:S(2)}, u32[]{:S(2)}) collective-permute-start(bf16[8,48,512]{2,1,0:T(8,128)(2,1)} %get-tuple-element.28), channel_id=1, source_target_pairs={{0,8},{1,9},{2,10},{3,11},{4,12},{5,13},{6,14},{7,15},{8,16},{9,17... | collective-permute-start | bytes 1179656 | tf_op jit(solution)/shard_map/ppermute | solution.py:276
  8.1 28.1 %collective-permute-start.4 = (bf16[8,48,512]{2,1,0:T(8,128)(2,1)}, bf16[8,48,512]{2,1,0:T(8,128)(2,1)S(1)}, u32[]{:S(2)}, u32[]{:S(2)}) collective-permute-start(bf16[8,48,512]{2,1,0:T(8,128)(2,1)} %get-tuple-element.29), channel_id=1, source_target_pairs={{0,16},{1,17},{2,18},{3,19},{4,20},{5,21},{6,22},{7,23},{8,24},{9,... | collective-permute-start | bytes 1179656 | tf_op jit(solution)/shard_map/ppermute | solution.py:276
  11.4 24.8 %collective-permute-start.5 = (bf16[8,48,512]{2,1,0:T(8,128)(2,1)}, bf16[8,48,512]{2,1,0:T(8,128)(2,1)S(1)}, u32[]{:S(2)}, u32[]{:S(2)}) collective-permute-start(bf16[8,48,512]{2,1,0:T(8,128)(2,1)} %get-tuple-element.30), channel_id=1, source_target_pairs={{0,24},{1,25},{2,26},{3,27},{4,28},{5,29},{6,30},{7,31},{8,0},{9,1... | collective-permute-start | bytes 1179656 | tf_op jit(solution)/shard_map/ppermute | solution.py:276
  31.1 23.5 %collective-permute-start = (bf16[8,48,512]{2,1,0:T(8,128)(2,1)}, bf16[8,48,512]{2,1,0:T(8,128)(2,1)S(1)}, u32[]{:S(2)}, u32[]{:S(2)}) collective-permute-start(bf16[8,48,512]{2,1,0:T(8,128)(2,1)} %get-tuple-element.25), channel_id=1, source_target_pairs={{0,32},{32,64},{64,96},{96,0},{1,33},{33,65},{65,97},{97,1},{2,34}... | collective-permute-start | bytes 1179656 | tf_op jit(solution)/shard_map/ppermute | solution.py:273
  32.5 22.2 %collective-permute-start.1 = (bf16[8,48,512]{2,1,0:T(8,128)(2,1)}, bf16[8,48,512]{2,1,0:T(8,128)(2,1)S(1)}, u32[]{:S(2)}, u32[]{:S(2)}) collective-permute-start(bf16[8,48,512]{2,1,0:T(8,128)(2,1)} %get-tuple-element.26), channel_id=1, source_target_pairs={{0,64},{32,96},{64,0},{96,32},{1,65},{33,97},{65,1},{97,33},{2,66}... | collective-permute-start | bytes 1179656 | tf_op jit(solution)/shard_map/ppermute | solution.py:273
  35.1 19.6 %collective-permute-start.2 = (bf16[8,48,512]{2,1,0:T(8,128)(2,1)}, bf16[8,48,512]{2,1,0:T(8,128)(2,1)S(1)}, u32[]{:S(2)}, u32[]{:S(2)}) collective-permute-start(bf16[8,48,512]{2,1,0:T(8,128)(2,1)} %get-tuple-element.27), channel_id=1, source_target_pairs={{0,96},{32,0},{64,32},{96,64},{1,97},{33,1},{65,33},{97,65},{2,98}... | collective-permute-start | bytes 1179656 | tf_op jit(solution)/shard_map/ppermute | solution.py:273
  54.9 5.2 %collective-permute-start.13 = (bf16[2,48,512]{2,1,0:T(8,128)(2,1)S(1)}, bf16[2,48,512]{2,1,0:T(8,128)(2,1)S(1)}, u32[]{:S(2)}, u32[]{:S(2)}) collective-permute-start(bf16[2,48,512]{2,1,0:T(8,128)(2,1)S(1)} %get-tuple-element.45), channel_id=1, source_target_pairs={{0,8},{1,9},{2,10},{3,11},{4,12},{5,13},{6,14},{7,15},{8,16},{9,17... | collective-permute-start | bytes 294920 | tf_op jit(solution)/shard_map/ppermute | solution.py:276
  55.3 6.0 %collective-permute-start.14 = (bf16[2,48,512]{2,1,0:T(8,128)(2,1)S(1)}, bf16[2,48,512]{2,1,0:T(8,128)(2,1)S(1)}, u32[]{:S(2)}, u32[]{:S(2)}) collective-permute-start(bf16[2,48,512]{2,1,0:T(8,128)(2,1)S(1)} %get-tuple-element.47), channel_id=1, source_target_pairs={{0,16},{1,17},{2,18},{3,19},{4,20},{5,21},{6,22},{7,23},{8,24},{9,... | collective-permute-start | bytes 294920 | tf_op jit(solution)/shard_map/ppermute | solution.py:276
  55.7 5.8 %collective-permute-start.15 = (bf16[2,48,512]{2,1,0:T(8,128)(2,1)S(1)}, bf16[2,48,512]{2,1,0:T(8,128)(2,1)S(1)}, u32[]{:S(2)}, u32[]{:S(2)}) collective-permute-start(bf16[2,48,512]{2,1,0:T(8,128)(2,1)S(1)} %get-tuple-element.46), channel_id=1, source_target_pairs={{0,24},{1,25},{2,26},{3,27},{4,28},{5,29},{6,30},{7,31},{8,0},{9,1... | collective-permute-start | bytes 294920 | tf_op jit(solution)/shard_map/ppermute | solution.py:276
  57.8 13.6 %collective-permute-start.6 = (bf16[2,4,48,512]{3,2,1,0:T(8,128)(2,1)}, bf16[2,4,48,512]{3,2,1,0:T(8,128)(2,1)S(1)}, u32[]{:S(2)}, u32[]{:S(2)}) collective-permute-start(bf16[2,4,48,512]{3,2,1,0:T(8,128)(2,1)} %get-tuple-element.33), channel_id=1, source_target_pairs={{0,32},{32,64},{64,96},{96,0},{1,33},{33,65},{65,97},{97,1},{2,34}... | collective-permute-start | bytes 1179656 | tf_op jit(solution)/shard_map/ppermute | solution.py:273
  61.7 8.1 %collective-permute-start.17 = (bf16[2,48,512]{2,1,0:T(8,128)(2,1)S(1)}, bf16[2,48,512]{2,1,0:T(8,128)(2,1)S(1)}, u32[]{:S(2)}, u32[]{:S(2)}) collective-permute-start(bf16[2,48,512]{2,1,0:T(8,128)(2,1)S(1)} %get-tuple-element.56), channel_id=1, source_target_pairs={{0,64},{32,96},{64,0},{96,32},{1,65},{33,97},{65,1},{97,33},{2,66}... | collective-permute-start | bytes 294920 | tf_op jit(solution)/shard_map/ppermute | solution.py:273
  61.8 8.0 %collective-permute-start.18 = (bf16[2,48,512]{2,1,0:T(8,128)(2,1)S(1)}, bf16[2,48,512]{2,1,0:T(8,128)(2,1)S(1)}, u32[]{:S(2)}, u32[]{:S(2)}) collective-permute-start(bf16[2,48,512]{2,1,0:T(8,128)(2,1)S(1)} %get-tuple-element.55), channel_id=1, source_target_pairs={{0,96},{32,0},{64,32},{96,64},{1,97},{33,1},{65,33},{97,65},{2,98}... | collective-permute-start | bytes 294920 | tf_op jit(solution)/shard_map/ppermute | solution.py:273
  64.4 7.0 %collective-permute-start.16 = (bf16[2,48,512]{2,1,0:T(8,128)(2,1)S(1)}, bf16[2,48,512]{2,1,0:T(8,128)(2,1)S(1)}, u32[]{:S(2)}, u32[]{:S(2)}) collective-permute-start(bf16[2,48,512]{2,1,0:T(8,128)(2,1)S(1)} %get-tuple-element.43), channel_id=1, source_target_pairs={{0,32},{32,64},{64,96},{96,0},{1,33},{33,65},{65,97},{97,1},{2,34}... | collective-permute-start | bytes 294920 | tf_op jit(solution)/shard_map/ppermute | solution.py:273
  64.4 10.6 %collective-permute-start.8 = (bf16[2,4,48,512]{3,2,1,0:T(8,128)(2,1)}, bf16[2,4,48,512]{3,2,1,0:T(8,128)(2,1)S(1)}, u32[]{:S(2)}, u32[]{:S(2)}) collective-permute-start(bf16[2,4,48,512]{3,2,1,0:T(8,128)(2,1)} %get-tuple-element.35), channel_id=1, source_target_pairs={{0,96},{32,0},{64,32},{96,64},{1,97},{33,1},{65,33},{97,65},{2,98}... | collective-permute-start | bytes 1179656 | tf_op jit(solution)/shard_map/ppermute | solution.py:273
  72.4 11.4 %collective-permute-start.7 = (bf16[4,48,512]{2,1,0:T(8,128)(2,1)S(1)}, bf16[4,48,512]{2,1,0:T(8,128)(2,1)S(1)}, u32[]{:S(2)}, u32[]{:S(2)}) collective-permute-start(bf16[4,48,512]{2,1,0:T(8,128)(2,1)S(1)} %fusion.1), channel_id=1, source_target_pairs={{0,32},{32,64},{64,96},{96,0},{1,33},{33,65},{65,97},{97,1},{2,34}... | collective-permute-start | bytes 589832 | tf_op jit(solution)/shard_map/ppermute | solution.py:273
  76.0 7.9 %collective-permute-start.10 = (bf16[4,48,512]{2,1,0:T(8,128)(2,1)S(1)}, bf16[4,48,512]{2,1,0:T(8,128)(2,1)S(1)}, u32[]{:S(2)}, u32[]{:S(2)}) collective-permute-start(bf16[4,48,512]{2,1,0:T(8,128)(2,1)S(1)} %fusion), channel_id=1, source_target_pairs={{0,96},{32,0},{64,32},{96,64},{1,97},{33,1},{65,33},{97,65},{2,98}... | collective-permute-start | bytes 589832 | tf_op jit(solution)/shard_map/ppermute | solution.py:273
  78.2 24.7 %copy-start = (bf16[2,48,512]{2,1,0:T(8,128)(2,1)}, bf16[2,48,512]{2,1,0:T(8,128)(2,1)S(1)}, u32[]{:S(2)}) copy-start(bf16[2,48,512]{2,1,0:T(8,128)(2,1)S(1)} %get-tuple-element.54.refs_4_) | copy-start | bytes 294916
  78.2 18.1 %collective-permute-start.19 = (bf16[2,48,512]{2,1,0:T(8,128)(2,1)S(1)}, bf16[2,48,512]{2,1,0:T(8,128)(2,1)S(1)}, u32[]{:S(2)}, u32[]{:S(2)}) collective-permute-start(bf16[2,48,512]{2,1,0:T(8,128)(2,1)S(1)} %get-tuple-element.53), channel_id=1, source_target_pairs={{0,2},{1,3},{2,4},{3,5},{4,6},{5,7},{6,0},{7,1},{8,10},{9,11},{10,... | collective-permute-start | bytes 294920 | tf_op jit(solution)/shard_map/ppermute | solution.py:276
  80.2 16.2 %collective-permute-start.20 = (bf16[2,48,512]{2,1,0:T(8,128)(2,1)S(1)}, bf16[2,48,512]{2,1,0:T(8,128)(2,1)S(1)}, u32[]{:S(2)}, u32[]{:S(2)}) collective-permute-start(bf16[2,48,512]{2,1,0:T(8,128)(2,1)S(1)} %get-tuple-element.52), channel_id=1, source_target_pairs={{0,4},{1,5},{2,6},{3,7},{4,0},{5,1},{6,2},{7,3},{8,12},{9,13},{10,... | collective-permute-start | bytes 294920 | tf_op jit(solution)/shard_map/ppermute | solution.py:276
  82.0 14.5 %collective-permute-start.21 = (bf16[2,48,512]{2,1,0:T(8,128)(2,1)S(1)}, bf16[2,48,512]{2,1,0:T(8,128)(2,1)S(1)}, u32[]{:S(2)}, u32[]{:S(2)}) collective-permute-start(bf16[2,48,512]{2,1,0:T(8,128)(2,1)S(1)} %get-tuple-element.41), channel_id=1, source_target_pairs={{0,6},{1,7},{2,0},{3,1},{4,2},{5,3},{6,4},{7,5},{8,14},{9,15},{10,... | collective-permute-start | bytes 294920 | tf_op jit(solution)/shard_map/ppermute | solution.py:276
  85.0 6.9 %collective-permute-start.9 = (bf16[2,48,512]{2,1,0:T(8,128)(2,1)S(1)}, bf16[2,48,512]{2,1,0:T(8,128)(2,1)S(1)}, u32[]{:S(2)}, u32[]{:S(2)}) collective-permute-start(bf16[2,48,512]{2,1,0:T(8,128)(2,1)S(1)} %get-tuple-element.58), channel_id=1, source_target_pairs={{0,2},{1,3},{2,4},{3,5},{4,6},{5,7},{6,0},{7,1},{8,10},{9,11},{10,... | collective-permute-start | bytes 294920 | tf_op jit(solution)/shard_map/ppermute | solution.py:276
  85.1 6.8 %collective-permute-start.11 = (bf16[2,48,512]{2,1,0:T(8,128)(2,1)S(1)}, bf16[2,48,512]{2,1,0:T(8,128)(2,1)S(1)}, u32[]{:S(2)}, u32[]{:S(2)}) collective-permute-start(bf16[2,48,512]{2,1,0:T(8,128)(2,1)S(1)} %get-tuple-element.49), channel_id=1, source_target_pairs={{0,4},{1,5},{2,6},{3,7},{4,0},{5,1},{6,2},{7,3},{8,12},{9,13},{10,... | collective-permute-start | bytes 294920 | tf_op jit(solution)/shard_map/ppermute | solution.py:276
  91.9 4.4 %collective-permute-start.12 = (bf16[2,48,512]{2,1,0:T(8,128)(2,1)S(1)}, bf16[2,48,512]{2,1,0:T(8,128)(2,1)S(1)}, u32[]{:S(2)}, u32[]{:S(2)}) collective-permute-start(bf16[2,48,512]{2,1,0:T(8,128)(2,1)S(1)} %get-tuple-element.48), channel_id=1, source_target_pairs={{0,6},{1,7},{2,0},{3,1},{4,2},{5,3},{6,4},{7,5},{8,14},{9,15},{10,... | collective-permute-start | bytes 294920 | tf_op jit(solution)/shard_map/ppermute | solution.py:276
  96.5 6.4 %collective-permute-start.22 = (bf16[8,48,512]{2,1,0:T(8,128)(2,1)S(1)}, bf16[8,48,512]{2,1,0:T(8,128)(2,1)S(1)}, u32[]{:S(2)}, u32[]{:S(2)}) collective-permute-start(bf16[8,48,512]{2,1,0:T(8,128)(2,1)S(1)} %fusion.6), channel_id=1, source_target_pairs={{0,1},{1,0},{2,3},{3,2},{4,5},{5,4},{6,7},{7,6},{8,9},{9,8},{10,11... | collective-permute-start | bytes 1179656 | tf_op jit(solution)/shard_map/ppermute | solution.py:276
  (12 other events, 89.2 us)

commit v3 on v2

v3 whole, which is shorter than its diff:
```python
import functools
import jax
import jax.numpy as jnp
from jax import lax
from jax.experimental import pallas as pl
from jax.experimental.pallas import tpu as pltpu
from jax.sharding import PartitionSpec as P

TAKE = 10
MORE = 4
ROOM = 64
LINE, CORES, TEAM, RING = 4, 2, 8, 4
VMEM = 28 * 2**20
ALL_VMEM = 58 * 2**20

f32, bf16, i32 = jnp.float32, jnp.bfloat16, jnp.int32
ANY = pl.BlockSpec(memory_space=pl.ANY)
HBM = pl.BlockSpec(memory_space=pltpu.HBM)


def where_am_i():
    sub = lax.axis_index("sub")
    return lax.axis_index("grp"), sub >> 3, (sub >> 1) & 3, sub & 1


def run(copies):
    for c in copies:
        c.start()
    for c in copies:
        c.wait()


def row_fetches(block, pulses_ref, rows, row_sem):
    width = rows.shape[2]
    return [
        pltpu.make_async_copy(pulses_ref.at[j, :, pl.ds(block * width, width)], rows.at[j], row_sem.at[j])
        for j in range(rows.shape[0])
    ]


def projected(o, foot, weights, rows):
    both = jnp.concatenate([rows[o], rows[foot[1, o]]], axis=0)
    return jnp.dot(weights[o], both, preferred_element_type=f32).astype(bf16)


def start_kernel(block, foot_ref, pulses_ref, weight_ref, *rest):
    outs, (foot, rows, weights, image, row_sem, sem, out_sem) = rest[:RING], rest[RING:]
    first = [pltpu.make_async_copy(foot_ref, foot, sem.at[0]), pltpu.make_async_copy(weight_ref, weights, sem.at[1])]
    copies = first + row_fetches(block, pulses_ref, rows, row_sem)
    run(copies)
    _, z, _, _ = where_am_i()
    sends = []
    for d in (1, 3, 2, 0):
        for j in range(TEAM):
            o = ((z + d) & 3) * TEAM + j
            image[d * TEAM + j] = projected(o, foot, weights, rows)
        sends.append(pltpu.make_async_copy(image.at[pl.ds(d * TEAM, TEAM)], outs[d], out_sem.at[d]))
        sends[-1].start()
    for copy in sends:
        copy.wait()


def start_images(block, foot, pulses, weight, width):
    owners, beams, depth = weight.shape
    return pl.pallas_call(
        functools.partial(start_kernel, block),
        in_specs=[HBM] * 3,
        out_specs=[ANY] * RING,
        out_shape=[jax.ShapeDtypeStruct((TEAM, beams, width), bf16)] * RING,
        scratch_shapes=[
            pltpu.SMEM(foot.shape, i32),
            pltpu.VMEM((owners, depth // 2, width), bf16),
            pltpu.VMEM((owners, beams, depth), bf16),
            pltpu.VMEM((owners, beams, width), bf16),
            pltpu.SemaphoreType.DMA((owners,)),
            pltpu.SemaphoreType.DMA((2,)),
            pltpu.SemaphoreType.DMA((RING,)),
        ],
        compiler_params=pltpu.CompilerParams(vmem_limit_bytes=ALL_VMEM),
        cost_estimate=pl.CostEstimate(flops=400_000_000, bytes_accessed=7 * 2**20, transcendentals=0),
        name="start",
    )(foot, pulses, weight)


def tree_kernel(joined, block, levels, *refs):
    if joined:
        part_refs, (index_ref, bank_ref), refs = refs[:RING], refs[RING:RING + 2], refs[RING + 2:]
        outs, refs = refs[:5], refs[5:]
    else:
        (foot_ref, pulses_ref, weight_ref, _, index_ref, bank_ref), refs = refs[:6], refs[6:]
        outs, refs = refs[:RING], refs[RING:]
    index, mats, image, acc, stage, sem, row_sem, mat_sem, out_sem = refs[:9]
    lists, refs = refs[9:9 + 2 * levels], refs[9 + 2 * levels:]
    images, beams, width = stage.shape[0], stage.shape[1], stage.shape[2]
    kinds = mats.shape[0]
    y, z, x, c = where_am_i()
    blocks = index.shape[3] // (RING * TEAM)

    index_copy = pltpu.make_async_copy(index_ref, index, sem.at[0])
    mat_copies = [pltpu.make_async_copy(bank_ref.at[k], mats.at[k], mat_sem.at[k]) for k in range(kinds)]
    if joined:
        feeds = [
            pltpu.make_async_copy(part_refs[d], image.at[0, pl.ds(d * TEAM, TEAM)], row_sem.at[d])
            for d in range(RING)
        ]
    else:
        foot, rows, weights = refs
        feeds = [
            pltpu.make_async_copy(foot_ref, foot, sem.at[1]),
            pltpu.make_async_copy(weight_ref, weights, sem.at[2]),
        ] + row_fetches(block, pulses_ref, rows, row_sem)
    for copy in [index_copy] + feeds + mat_copies:
        copy.start()

    def kind_of(level, which, i):
        if joined:
            owner = z * TEAM + i % TEAM
            column = (((z - i // TEAM) & 3) * TEAM + x * CORES + c) * blocks + block
        else:
            owner = i
            column = ((z * LINE + x) * CORES + c) * blocks + block
        return index[level, owner, which, column]

    def sort_level(level):
        counts, uses = lists[2 * level:2 * level + 2]
        for k in range(kinds):
            counts[k] = 0
            for i in range(TAKE):
                uses[k * ROOM + i] = images
        for which in range(2):
            for i in range(images):
                k = kind_of(level, which, i)
                n = counts[k]
                uses[k * ROOM + n] = which * ROOM + i
                counts[k] = n + 1

    def multiply(level, k, taken):
        which = [v >> 6 for v in taken]
        dest = [v & (ROOM - 1) for v in taken]
        many = jnp.concatenate(
            [image[level % 2, jnp.bitwise_xor(d, w << level)] for d, w in zip(dest, which)], axis=0)
        out = jnp.dot(many, mats[k], preferred_element_type=f32)
        for i, (d, w) in enumerate(zip(dest, which)):
            acc[w, d] = out[i * beams:(i + 1) * beams]

    def merge(level):
        counts, uses = lists[2 * level:2 * level + 2]
        for k in range(kinds):
            if level == 0:
                mat_copies[k].wait()
            multiply(level, k, [uses[k * ROOM + i] for i in range(TAKE)])

        def rest(k, carry):
            n = counts[k]

            def more(t, carry):
                first = TAKE + t * MORE
                multiply(level, k, [
                    jnp.where(first + i < n, uses[k * ROOM + first + i], images) for i in range(MORE)])
                return carry

            return lax.fori_loop(0, (jnp.maximum(n - TAKE, 0) + (MORE - 1)) >> 2, more, carry)

        lax.fori_loop(0, kinds, rest, 0)
        for d in range(images):
            merged = (acc[0, d] + acc[1, d]).astype(bf16)
            if level + 1 < levels:
                image[(level + 1) % 2, d] = merged
            else:
                team, xo, co = d // TEAM, (d // CORES) % LINE, d % CORES
                if joined:
                    place = ((z - team - y) & 3) * TEAM + ((xo - x) & 3) * CORES + co
                else:
                    place = ((xo - y) & 3) * TEAM + ((team - z) & 3) * CORES + co
                stage[place] = merged

    index_copy.wait()
    sort_level(0)
    for copy in feeds:
        copy.wait()
    if not joined:
        for o in range(images):
            image[0, o] = projected(o, foot, weights, rows)
    for level in range(levels):
        if level + 1 < levels:
            sort_level(level + 1)
        merge(level)

    half = TEAM // 2
    if joined:
        moves = [
            (2 * TEAM, half, outs[0].at[0]), (TEAM + half, half, outs[0].at[1]),
            (2 * TEAM + half, half, outs[1].at[0]), (3 * TEAM, half, outs[1].at[1]),
            (TEAM, half, outs[2]), (3 * TEAM + half, half, outs[3]), (0, TEAM, outs[4]),
        ]
    else:
        moves = [(r * TEAM, TEAM, outs[r]) for r in (2, 1, 3, 0)]
    run([
        pltpu.make_async_copy(stage.at[pl.ds(s, n)], ref, out_sem.at[i]) for i, (s, n, ref) in enumerate(moves)
    ])


def trees(joined, block, index, bank, beams, feeds):
    kinds, width, _ = bank.shape
    levels, images = index.shape[:2]
    whole = jax.ShapeDtypeStruct((TEAM, beams, width), bf16)
    pair = jax.ShapeDtypeStruct((2, TEAM // 2, beams, width), bf16)
    piece = jax.ShapeDtypeStruct((TEAM // 2, beams, width), bf16)
    scratch = [
        pltpu.SMEM(index.shape, i32),
        pltpu.VMEM(bank.shape, bf16),
        pltpu.VMEM((2, images + TEAM, beams, width), bf16),
        pltpu.VMEM((2, images + 1, beams, width), f32),
        pltpu.VMEM((images, beams, width), bf16),
        pltpu.SemaphoreType.DMA((3,)),
        pltpu.SemaphoreType.DMA((images,)),
        pltpu.SemaphoreType.DMA((kinds,)),
        pltpu.SemaphoreType.DMA((7,)),
    ]
    for _ in range(levels):
        scratch += [pltpu.SMEM((n,), i32) for n in (kinds, kinds * ROOM + TAKE)]
    if not joined:
        foot, pulses, weight, _ = feeds
        owners, _, depth = weight.shape
        scratch += [
            pltpu.SMEM(foot.shape, i32),
            pltpu.VMEM((owners, depth // 2, width), bf16),
            pltpu.VMEM((owners, beams, depth), bf16),
        ]
    out_shape = [pair, pair, piece, piece, whole] if joined else [whole] * RING
    return pl.pallas_call(
        functools.partial(tree_kernel, joined, block, levels),
        in_specs=[ANY if joined else HBM] * len(feeds) + [HBM] * 2,
        out_specs=[ANY] * len(out_shape),
        out_shape=out_shape,
        scratch_shapes=scratch,
        compiler_params=pltpu.CompilerParams(vmem_limit_bytes=VMEM if joined else ALL_VMEM),
        cost_estimate=pl.CostEstimate(flops=9_000_000_000, bytes_accessed=11 * 2**20, transcendentals=0),
        name="joined_trees" if joined else "trees",
    )(*feeds, index, bank)


def lay_kernel(*refs):
    mine, (other, out_ref, slab, sem, out_sem) = refs[:LINE], refs[LINE:]
    _, _, x, c = where_am_i()
    _, blocks, _, width = other.shape
    copies = []
    for d in range(LINE):
        for b in range(blocks):
            for source, core in ((mine[d].at[b, c], c), (other.at[d, b], 1 - c)):
                at = ((((x - d) & 3) * CORES + core) * blocks + b) * width
                copies.append(pltpu.make_async_copy(
                    source, slab.at[:, pl.ds(pl.multiple_of(at, width), width)], sem.at[len(copies)]))
    run(copies)
    run([pltpu.make_async_copy(slab, out_ref, out_sem)])


def total(*parts):
    out = parts[0].astype(f32)
    for part in parts[1:]:
        out = out + part.astype(f32)
    return out.astype(bf16)


def turn(pieces, shift):
    return [lax.select_n((shift - d) & 3, *pieces) for d in range(len(pieces))]


def body(pulses, footprint, proj_weight, bank, merge_index):
    held = pulses[0]
    width = bank.shape[1]
    owners, beams, _ = proj_weight.shape
    y, z, x, c = where_am_i()
    foot = footprint.T
    index = merge_index[:, 0].transpose(0, 1, 3, 2)
    held, foot, proj_weight, bank, index = [
        pltpu.with_memory_space_constraint(a, pltpu.HBM) for a in (held, foot, proj_weight, bank, index)
    ]

    def along_y(value, d):
        return lax.ppermute(value, "grp", [(i, (i + d) % RING) for i in range(RING)])

    def along_sub(value, move):
        return lax.ppermute(value, "sub", [(i, move(i >> 3, (i >> 1) & 3, i & 1)) for i in range(owners)])

    def along_z(value, d):
        return along_sub(value, lambda zz, xx, cc: ((zz + d) % RING) * TEAM + xx * CORES + cc)

    def along_x(value, d):
        return along_sub(value, lambda zz, xx, cc: zz * TEAM + ((xx + d) % LINE) * CORES + cc)

    def exchange(pieces, along):
        return [pieces[0]] + [along(pieces[d], d) for d in range(1, len(pieces))]

    begun = start_images(0, foot, held, proj_weight, width)
    spread = exchange(begun, along_z)
    sent = trees(False, 1, index, bank, beams, (foot, held, proj_weight, begun[0]))
    got = exchange(sent, along_y)
    to_up, to_down, keep_up, keep_down, own = trees(True, 0, index, bank, beams, tuple(spread))
    got, own = lax.optimization_barrier((got, own))
    from_down, from_up = along_y(to_up, 1), along_y(to_down, -1)
    pieces = [total(*[g[r * CORES:(r + 1) * CORES] for g in got]) for r in range(RING)]
    pieces = exchange(pieces, along_z)
    from_down, from_up, pieces = lax.optimization_barrier((from_down, from_up, pieces))
    last_down = along_y(total(from_down[0], keep_up), 1)
    last_up = along_y(total(from_up[0], keep_down), -1)
    pieces = exchange(turn(pieces, z - y), along_y)
    last_down, last_up, pieces = lax.optimization_barrier((last_down, last_up, pieces))
    half = TEAM // 2

    summed = []
    for r in range(LINE):
        low = r * CORES < half
        lo = r * CORES - (0 if low else half)
        near, far = (last_down, from_up[1]) if low else (last_up, from_down[1])
        summed.append(total(own[r * CORES:(r + 1) * CORES], near[lo:lo + CORES], far[lo:lo + CORES]))

    mine = exchange([jnp.stack(both) for both in zip(summed, turn(pieces, y - x))], along_x)
    other = jnp.stack([jnp.where(c == 0, piece[:, 1], piece[:, 0]) for piece in mine])
    other = along_sub(other, lambda zz, xx, cc: zz * TEAM + xx * CORES + 1 - cc)

    return pl.pallas_call(
        lay_kernel,
        in_specs=[ANY] * (LINE + 1),
        out_specs=ANY,
        out_shape=jax.ShapeDtypeStruct((beams, LINE * CORES * 2 * width), bf16),
        scratch_shapes=[
            pltpu.VMEM((beams, LINE * CORES * 2 * width), bf16),
            pltpu.SemaphoreType.DMA((2 * CORES * LINE,)),
            pltpu.SemaphoreType.DMA,
        ],
        compiler_params=pltpu.CompilerParams(vmem_limit_bytes=4 * 2**20),
        name="lay",
    )(*mine, other)


def solution(mesh):
    placed = (P("grp", None, None, "sub"), P(), P(), P(), P(None, "grp", None, None, None))
    return jax.shard_map(
        body, mesh=mesh, in_specs=placed, out_specs=P("sub", "grp"), check_vma=False
    )
```

time: 106 us -> 89.6 us (0.85)
  waiting for transfers between devices: 21.2 us -> 17 us
  Pallas kernels: 43.8 us -> 39.6 us
  other arithmetic: 3.63 us -> 0.78 us
  starting transfers between devices: 34.9 us -> 32.1 us
  local copies, waits for them, and re-layouts: 2.25 us -> 0.02 us
    ppermute x13 -> x10, starting transfers between devices: 21.5 us -> 18.2 us  [along_sub(): lax.ppermute(value, 'sub', [(i, move(i >> 3, i >> 1 & 3, i & 1)) for i in...]
    convert_element_type x4 -> x3, other arithmetic: 3.3 us -> 0.31 us  [total(): return out.astype(bf16)]
    pallas_call x2, Pallas kernels: 36 us -> 33.2 us  [trees(): pl.pallas_call(functools.partial(tree_kernel, joined, block, levels), in_...]
    ppermute x13 -> x10, waiting for transfers between devices: 14.3 us -> 11.7 us  [along_sub(): lax.ppermute(value, 'sub', [(i, move(i >> 3, i >> 1 & 3, i & 1)) for i in...]
    unnamed x26 -> x4, local copies, waits for them, and re-layouts: 2.25 us -> 0.01 us
    ppermute x10, waiting for transfers between devices: 6.84 us -> 5.25 us  [along_y(): lax.ppermute(value, 'grp', [(i, (i + d) % RING) for i in range(RING)])]
    pallas_call x2, Pallas kernels: 7.83 us -> 6.39 us  [the longest x1 5.15 us: start_images(): pl.pallas_call(functools.partial(start_kernel, block), in_specs=[HBM] * 3...]
  transfers between devices with their start and end apart: 23 -> 20, of which waited for: 9 -> 11; matrix products, arithmetic and copies ran while one was open for 3% -> 0% of each run, Pallas kernels for 34% -> 37%
where the time goes in v3:
time: 89.6 us; the launch traced here: 89.8 us
  Pallas kernels  39.6 us (44%)
  starting transfers between devices  32.1 us (36%)
  waiting for transfers between devices  17 us (19%)
    pallas_call x2, Pallas kernels, trees(): pl.pallas_call(functools.partial(tree_kernel, joined, block, levels), in_...  33.2 us
    ppermute x10, starting transfers between devices, along_sub(): lax.ppermute(value, 'sub', [(i, move(i >> 3, i >> 1 & 3, i & 1)) for i in...  18.2 us
    ppermute x10, starting transfers between devices, along_y(): lax.ppermute(value, 'grp', [(i, (i + d) % RING) for i in range(RING)])  13.9 us
    ppermute x10, waiting for transfers between devices, along_sub(): lax.ppermute(value, 'sub', [(i, move(i >> 3, i >> 1 & 3, i & 1)) for i in...  11.7 us
    ppermute x10, waiting for transfers between devices, along_y(): lax.ppermute(value, 'grp', [(i, (i + d) % RING) for i in range(RING)])  5.25 us
    pallas_call x1, Pallas kernels, start_images(): pl.pallas_call(functools.partial(start_kernel, block), in_specs=[HBM] * 3...  5.15 us
  transfers between devices with their start and end apart: 20, of which 11 were waited for; matrix products, arithmetic and copies ran while one was open for 0% of the time, Pallas kernels for 37%

profile of v3, /device:TPU:1, one launch (start us, length us, event | category | flops | bytes accessed | tf_op | source)
XLA Modules:
  0.0 89.8 jit_solution(4802818607471416255)
XLA Ops:
  0.0 5.2 %start.1 = (bf16[8,48,512]{2,1,0:T(8,128)(2,1)}, bf16[8,48,512]{2,1,0:T(8,128)(2,1)}, bf16[8,48,512]{2,1,0:T(8,128)(2,1)}, bf16[8,48,512]{2,1,0:T(8,128)(2,1)}) custom-call(s32[2,32]{1,0:T(2,128)} %bitcast.55, bf16[32,128,1024]{2,1,0:T(8,128)(2,1)} %bitcast.53, bf16[32,48,256]{2,1,0:T(8,128)(2,1)} %refs_2_.1), custom_call_target="tpu_custom_call" | custom-call | flops 400000000 | bytes 7340032 | tf_op jit(solution)/shard_map/start/pallas_call | solution.py:65
  5.2 2.5 %collective-permute-start.3 = (bf16[8,48,512]{2,1,0:T(8,128)(2,1)}, bf16[8,48,512]{2,1,0:T(8,128)(2,1)S(1)}, u32[]{:S(2)}, u32[]{:S(2)}) collective-permute-start(bf16[8,48,512]{2,1,0:T(8,128)(2,1)} %get-tuple-element.40), channel_id=1, source_target_pairs={{0,8},{1,9},{2,10},{3,11},{4,12},{5,13},{6,14},{7,15},{8,16},{9,17... | collective-permute-start | bytes 1179656 | tf_op jit(solution)/shard_map/ppermute | solution.py:284
  7.7 3.3 %collective-permute-start.4 = (bf16[8,48,512]{2,1,0:T(8,128)(2,1)}, bf16[8,48,512]{2,1,0:T(8,128)(2,1)S(1)}, u32[]{:S(2)}, u32[]{:S(2)}) collective-permute-start(bf16[8,48,512]{2,1,0:T(8,128)(2,1)} %get-tuple-element.41), channel_id=1, source_target_pairs={{0,16},{1,17},{2,18},{3,19},{4,20},{5,21},{6,22},{7,23},{8,24},{9,... | collective-permute-start | bytes 1179656 | tf_op jit(solution)/shard_map/ppermute | solution.py:284
  11.7 17.4 %trees.1 = (bf16[8,48,512]{2,1,0:T(8,128)(2,1)}, bf16[8,48,512]{2,1,0:T(8,128)(2,1)}, bf16[8,48,512]{2,1,0:T(8,128)(2,1)}, bf16[8,48,512]{2,1,0:T(8,128)(2,1)}) custom-call(s32[2,32]{1,0:T(2,128)} %bitcast.56, bf16[32,128,1024]{2,1,0:T(8,128)(2,1)} %bitcast.54, bf16[32,48,256]{2,1,0:T(8,128)(2,1)} %refs_2_.1, ...), custom_call_target="tpu_custom_call" | custom-call | flops 8999999488 | bytes 11534336 | tf_op jit(solution)/shard_map/trees/pallas_call | solution.py:231
  29.1 1.1 %collective-permute-start = (bf16[8,48,512]{2,1,0:T(8,128)(2,1)}, bf16[8,48,512]{2,1,0:T(8,128)(2,1)S(1)}, u32[]{:S(2)}, u32[]{:S(2)}) collective-permute-start(bf16[8,48,512]{2,1,0:T(8,128)(2,1)} %get-tuple-element.37), channel_id=1, source_target_pairs={{0,32},{32,64},{64,96},{96,0},{1,33},{33,65},{65,97},{97,1},{2,34}... | collective-permute-start | bytes 1179656 | tf_op jit(solution)/shard_map/ppermute | solution.py:281
  30.2 2.4 %collective-permute-start.1 = (bf16[8,48,512]{2,1,0:T(8,128)(2,1)}, bf16[8,48,512]{2,1,0:T(8,128)(2,1)S(1)}, u32[]{:S(2)}, u32[]{:S(2)}) collective-permute-start(bf16[8,48,512]{2,1,0:T(8,128)(2,1)} %get-tuple-element.38), channel_id=1, source_target_pairs={{0,64},{32,96},{64,0},{96,32},{1,65},{33,97},{65,1},{97,33},{2,66}... | collective-permute-start | bytes 1179656 | tf_op jit(solution)/shard_map/ppermute | solution.py:281
  32.6 1.3 %collective-permute-start.2 = (bf16[8,48,512]{2,1,0:T(8,128)(2,1)}, bf16[8,48,512]{2,1,0:T(8,128)(2,1)S(1)}, u32[]{:S(2)}, u32[]{:S(2)}) collective-permute-start(bf16[8,48,512]{2,1,0:T(8,128)(2,1)} %get-tuple-element.39), channel_id=1, source_target_pairs={{0,96},{32,0},{64,32},{96,64},{1,97},{33,1},{65,33},{97,65},{2,98}... | collective-permute-start | bytes 1179656 | tf_op jit(solution)/shard_map/ppermute | solution.py:281
  33.9 15.8 %joined_trees.1 = (bf16[2,4,48,512]{3,2,1,0:T(8,128)(2,1)S(1)}, bf16[2,4,48,512]{3,2,1,0:T(8,128)(2,1)S(1)}, bf16[4,48,512]{2,1,0:T(8,128)(2,1)S(1)}, bf16[4,48,...) custom-call(bf16[8,48,512]{2,1,0:T(8,128)(2,1)S(1)} %copy-done, bf16[8,48,512]{2,1,0:T(8,128)(2,1)S(1)} %collective-permute-done.3.refs_1_, ...), custom_call_target="tpu_custom_call" | custom-call | flops 8999999488 | bytes 11534336 | tf_op jit(solution)/shard_map/joined_trees/pallas_call | solution.py:231
  49.8 2.7 %collective-permute-start.7 = (bf16[2,4,48,512]{3,2,1,0:T(8,128)(2,1)S(1)}, bf16[2,4,48,512]{3,2,1,0:T(8,128)(2,1)S(1)}, u32[]{:S(2)}, u32[]{:S(2)}) collective-permute-start(bf16[2,4,48,512]{3,2,1,0:T(8,128)(2,1)S(1)} %get-tuple-element.46), channel_id=1, source_target_pairs={{0,96},{32,0},{64,32},{96,64},{1,97},{33,1},{65,33},{97,65},{2,98}... | collective-permute-start | bytes 1179656 | tf_op jit(solution)/shard_map/ppermute | solution.py:281
  52.8 1.5 %collective-permute-start.8 = (bf16[2,48,512]{2,1,0:T(8,128)(2,1)S(1)}, bf16[2,48,512]{2,1,0:T(8,128)(2,1)S(1)}, u32[]{:S(2)}, u32[]{:S(2)}) collective-permute-start(bf16[2,48,512]{2,1,0:T(8,128)(2,1)S(1)} %get-tuple-element.67), channel_id=1, source_target_pairs={{0,8},{1,9},{2,10},{3,11},{4,12},{5,13},{6,14},{7,15},{8,16},{9,17... | collective-permute-start | bytes 294920 | tf_op jit(solution)/shard_map/ppermute | solution.py:284
  54.8 1.8 %collective-permute-done.10 = bf16[2,48,512]{2,1,0:T(8,128)(2,1)S(1)} collective-permute-done((bf16[2,48,512]{2,1,0:T(8,128)(2,1)S(1)}, bf16[2,48,512]{2,1,0:T(8,128)(2,1)S(1)}, u32[]{:S(2)}, u32[]{:S(2)}) %collective-permute-start.10) | collective-permute-done | bytes 98336 | tf_op jit(solution)/shard_map/ppermute | solution.py:284
  56.5 1.3 %collective-permute-done.8 = bf16[2,48,512]{2,1,0:T(8,128)(2,1)S(1)} collective-permute-done((bf16[2,48,512]{2,1,0:T(8,128)(2,1)S(1)}, bf16[2,48,512]{2,1,0:T(8,128)(2,1)S(1)}, u32[]{:S(2)}, u32[]{:S(2)}) %collective-permute-start.8) | collective-permute-done | bytes 98336 | tf_op jit(solution)/shard_map/ppermute | solution.py:284
  57.8 1.4 %collective-permute-done.9 = bf16[2,48,512]{2,1,0:T(8,128)(2,1)S(1)} collective-permute-done((bf16[2,48,512]{2,1,0:T(8,128)(2,1)S(1)}, bf16[2,48,512]{2,1,0:T(8,128)(2,1)S(1)}, u32[]{:S(2)}, u32[]{:S(2)}) %collective-permute-start.9) | collective-permute-done | bytes 98336 | tf_op jit(solution)/shard_map/ppermute | solution.py:284
  59.6 2.5 %collective-permute-start.12 = (bf16[4,48,512]{2,1,0:T(8,128)(2,1)S(1)}, bf16[4,48,512]{2,1,0:T(8,128)(2,1)S(1)}, u32[]{:S(2)}, u32[]{:S(2)}) collective-permute-start(bf16[4,48,512]{2,1,0:T(8,128)(2,1)S(1)} %fusion), channel_id=1, source_target_pairs={{0,96},{32,0},{64,32},{96,64},{1,97},{33,1},{65,33},{97,65},{2,98}... | collective-permute-start | bytes 589832 | tf_op jit(solution)/shard_map/ppermute | solution.py:281
  62.3 3.8 %collective-permute-start.14 = (bf16[2,48,512]{2,1,0:T(8,128)(2,1)S(1)}, bf16[2,48,512]{2,1,0:T(8,128)(2,1)S(1)}, u32[]{:S(2)}, u32[]{:S(2)}) collective-permute-start(bf16[2,48,512]{2,1,0:T(8,128)(2,1)S(1)} %get-tuple-element.80), channel_id=1, source_target_pairs={{0,64},{32,96},{64,0},{96,32},{1,65},{33,97},{65,1},{97,33},{2,66}... | collective-permute-start | bytes 294920 | tf_op jit(solution)/shard_map/ppermute | solution.py:281
  66.1 3.5 %collective-permute-done.13 = bf16[2,48,512]{2,1,0:T(8,128)(2,1)S(1)} collective-permute-done((bf16[2,48,512]{2,1,0:T(8,128)(2,1)S(1)}, bf16[2,48,512]{2,1,0:T(8,128)(2,1)S(1)}, u32[]{:S(2)}, u32[]{:S(2)}) %collective-permute-start.13) | collective-permute-done | bytes 98336 | tf_op jit(solution)/shard_map/ppermute | solution.py:281
  70.3 0.7 collective-permute-done.15
  72.1 2.1 %collective-permute-start.17 = (bf16[2,2,48,512]{3,2,1,0:T(8,128)(2,1)S(1)}, bf16[2,2,48,512]{3,2,1,0:T(8,128)(2,1)S(1)}, u32[]{:S(2)}, u32[]{:S(2)}) collective-permute-start(bf16[2,2,48,512]{3,2,1,0:T(8,128)(2,1)S(1)} %pad_maximum_fusion.3), channel_id=1, source_target_pairs={{0,4},{1,5},{2,6},{3,7},{4,0},{5,1},{6,2},{7,3},{8,12},{9,13},{10,... | collective-permute-start | bytes 589832 | tf_op jit(solution)/shard_map/ppermute | solution.py:284
  74.3 1.7 %collective-permute-done.18 = bf16[2,2,48,512]{3,2,0,1:T(8,128)(2,1)S(1)} collective-permute-done((bf16[2,2,48,512]{3,2,0,1:T(8,128)(2,1)S(1)}, bf16[2,2,48,512]{3,2,0,1:T(8,128)(2,1)S(1)}, u32[]{:S(2)}, u32[]{:S(2)}) %collective-permute-start.18) | collective-permute-done | bytes 196640 | tf_op jit(solution)/shard_map/ppermute | solution.py:284
  75.9 2.3 %collective-permute-done.17.refs_2_ = bf16[2,2,48,512]{3,2,1,0:T(8,128)(2,1)S(1)} collective-permute-done((bf16[2,2,48,512]{3,2,1,0:T(8,128)(2,1)S(1)}, bf16[2,2,48,512]{3,2,1,0:T(8,128)(2,1)S(1)}, u32[]{:S(2)}, u32[]{:S(2)}) %collective-permute-start.17) | collective-permute-done | bytes 196640 | tf_op jit(solution)/shard_map/ppermute | solution.py:284
  78.2 2.1 %collective-permute-done.16.refs_1_ = bf16[2,2,48,512]{3,2,1,0:T(8,128)(2,1)S(1)} collective-permute-done((bf16[2,2,48,512]{3,2,1,0:T(8,128)(2,1)S(1)}, bf16[2,2,48,512]{3,2,1,0:T(8,128)(2,1)S(1)}, u32[]{:S(2)}, u32[]{:S(2)}) %collective-permute-start.16) | collective-permute-done | bytes 196640 | tf_op jit(solution)/shard_map/ppermute | solution.py:284
  80.4 6.7 %collective-permute-start.19 = (bf16[4,2,48,512]{3,2,1,0:T(8,128)(2,1)S(1)}, bf16[4,2,48,512]{3,2,1,0:T(8,128)(2,1)S(1)}, u32[]{:S(2)}, u32[]{:S(2)}) collective-permute-start(bf16[4,2,48,512]{3,2,1,0:T(8,128)(2,1)S(1)} %pad_maximum_fusion), channel_id=1, source_target_pairs={{0,1},{1,0},{2,3},{3,2},{4,5},{5,4},{6,7},{7,6},{8,9},{9,8},{10,11... | collective-permute-start | bytes 1179656 | tf_op jit(solution)/shard_map/ppermute | solution.py:284
  87.1 1.3 %collective-permute-done.19.refs_4_ = bf16[4,2,48,512]{3,2,1,0:T(8,128)(2,1)S(1)} collective-permute-done((bf16[4,2,48,512]{3,2,1,0:T(8,128)(2,1)S(1)}, bf16[4,2,48,512]{3,2,1,0:T(8,128)(2,1)S(1)}, u32[]{:S(2)}, u32[]{:S(2)}) %collective-permute-start.19) | collective-permute-done | bytes 393248 | tf_op jit(solution)/shard_map/ppermute | solution.py:284
  88.4 1.2 %lay.1 = bf16[48,8192]{1,0:T(8,128)(2,1)} custom-call(bf16[2,2,48,512]{3,2,1,0:T(8,128)(2,1)S(1)} %pad_maximum_fusion.1.refs_0_, bf16[2,2,48,512]{3,2,1,0:T(8,128)(2,1)S(1)} %collective-permute-done.16.refs_1_, bf16[2,2,48,512]{3,2,1,0:T(8,128)(2,1)S(1)} %collective-permute-done.17.refs_2_, bf16[2,2,48,512]{3,2,1,0:T(8,128)(2,1)S(1)} %copy.8.refs_3_, ...), custom_call_target="tpu_custom_call" | custom-call | tf_op jit(solution)/shard_map/lay/pallas_call | solution.py:322
  (40 shorter events, 4.2 us)
Async XLA Ops:
  5.2 27.4 %collective-permute-start.3 = (bf16[8,48,512]{2,1,0:T(8,128)(2,1)}, bf16[8,48,512]{2,1,0:T(8,128)(2,1)S(1)}, u32[]{:S(2)}, u32[]{:S(2)}) collective-permute-start(bf16[8,48,512]{2,1,0:T(8,128)(2,1)} %get-tuple-element.40), channel_id=1, source_target_pairs={{0,8},{1,9},{2,10},{3,11},{4,12},{5,13},{6,14},{7,15},{8,16},{9,17... | collective-permute-start | bytes 1179656 | tf_op jit(solution)/shard_map/ppermute | solution.py:284
  7.7 26.2 %collective-permute-start.4 = (bf16[8,48,512]{2,1,0:T(8,128)(2,1)}, bf16[8,48,512]{2,1,0:T(8,128)(2,1)S(1)}, u32[]{:S(2)}, u32[]{:S(2)}) collective-permute-start(bf16[8,48,512]{2,1,0:T(8,128)(2,1)} %get-tuple-element.41), channel_id=1, source_target_pairs={{0,16},{1,17},{2,18},{3,19},{4,20},{5,21},{6,22},{7,23},{8,24},{9,... | collective-permute-start | bytes 1179656 | tf_op jit(solution)/shard_map/ppermute | solution.py:284
  11.0 22.9 %collective-permute-start.5 = (bf16[8,48,512]{2,1,0:T(8,128)(2,1)}, bf16[8,48,512]{2,1,0:T(8,128)(2,1)S(1)}, u32[]{:S(2)}, u32[]{:S(2)}) collective-permute-start(bf16[8,48,512]{2,1,0:T(8,128)(2,1)} %get-tuple-element.42), channel_id=1, source_target_pairs={{0,24},{1,25},{2,26},{3,27},{4,28},{5,29},{6,30},{7,31},{8,0},{9,1... | collective-permute-start | bytes 1179656 | tf_op jit(solution)/shard_map/ppermute | solution.py:284
  11.7 22.2 %copy-start = (bf16[8,48,512]{2,1,0:T(8,128)(2,1)S(1)}, bf16[8,48,512]{2,1,0:T(8,128)(2,1)}, u32[]{:S(2)}) copy-start(bf16[8,48,512]{2,1,0:T(8,128)(2,1)} %get-tuple-element.35.refs_3_.refs_0_) | copy-start | bytes 1179652
  29.1 23.4 %collective-permute-start = (bf16[8,48,512]{2,1,0:T(8,128)(2,1)}, bf16[8,48,512]{2,1,0:T(8,128)(2,1)S(1)}, u32[]{:S(2)}, u32[]{:S(2)}) collective-permute-start(bf16[8,48,512]{2,1,0:T(8,128)(2,1)} %get-tuple-element.37), channel_id=1, source_target_pairs={{0,32},{32,64},{64,96},{96,0},{1,33},{33,65},{65,97},{97,1},{2,34}... | collective-permute-start | bytes 1179656 | tf_op jit(solution)/shard_map/ppermute | solution.py:281
  30.2 22.3 %collective-permute-start.1 = (bf16[8,48,512]{2,1,0:T(8,128)(2,1)}, bf16[8,48,512]{2,1,0:T(8,128)(2,1)S(1)}, u32[]{:S(2)}, u32[]{:S(2)}) collective-permute-start(bf16[8,48,512]{2,1,0:T(8,128)(2,1)} %get-tuple-element.38), channel_id=1, source_target_pairs={{0,64},{32,96},{64,0},{96,32},{1,65},{33,97},{65,1},{97,33},{2,66}... | collective-permute-start | bytes 1179656 | tf_op jit(solution)/shard_map/ppermute | solution.py:281
  32.6 19.9 %copy-start.1 = (bf16[8,48,512]{2,1,0:T(8,128)(2,1)S(1)}, bf16[8,48,512]{2,1,0:T(8,128)(2,1)}, u32[]{:S(2)}) copy-start(bf16[8,48,512]{2,1,0:T(8,128)(2,1)} %get-tuple-element.47) | copy-start | bytes 1179652
  32.6 19.9 %collective-permute-start.2 = (bf16[8,48,512]{2,1,0:T(8,128)(2,1)}, bf16[8,48,512]{2,1,0:T(8,128)(2,1)S(1)}, u32[]{:S(2)}, u32[]{:S(2)}) collective-permute-start(bf16[8,48,512]{2,1,0:T(8,128)(2,1)} %get-tuple-element.39), channel_id=1, source_target_pairs={{0,96},{32,0},{64,32},{96,64},{1,97},{33,1},{65,33},{97,65},{2,98}... | collective-permute-start | bytes 1179656 | tf_op jit(solution)/shard_map/ppermute | solution.py:281
  49.7 9.8 %collective-permute-start.6 = (bf16[2,4,48,512]{3,2,1,0:T(8,128)(2,1)S(1)}, bf16[2,4,48,512]{3,2,1,0:T(8,128)(2,1)S(1)}, u32[]{:S(2)}, u32[]{:S(2)}) collective-permute-start(bf16[2,4,48,512]{3,2,1,0:T(8,128)(2,1)S(1)} %get-tuple-element.45), channel_id=1, source_target_pairs={{0,32},{32,64},{64,96},{96,0},{1,33},{33,65},{65,97},{97,1},{2,34}... | collective-permute-start | bytes 1179656 | tf_op jit(solution)/shard_map/ppermute | solution.py:281
  49.8 9.7 %collective-permute-start.7 = (bf16[2,4,48,512]{3,2,1,0:T(8,128)(2,1)S(1)}, bf16[2,4,48,512]{3,2,1,0:T(8,128)(2,1)S(1)}, u32[]{:S(2)}, u32[]{:S(2)}) collective-permute-start(bf16[2,4,48,512]{3,2,1,0:T(8,128)(2,1)S(1)} %get-tuple-element.46), channel_id=1, source_target_pairs={{0,96},{32,0},{64,32},{96,64},{1,97},{33,1},{65,33},{97,65},{2,98}... | collective-permute-start | bytes 1179656 | tf_op jit(solution)/shard_map/ppermute | solution.py:281
  52.7 3.8 %collective-permute-start.10 = (bf16[2,48,512]{2,1,0:T(8,128)(2,1)S(1)}, bf16[2,48,512]{2,1,0:T(8,128)(2,1)S(1)}, u32[]{:S(2)}, u32[]{:S(2)}) collective-permute-start(bf16[2,48,512]{2,1,0:T(8,128)(2,1)S(1)} %get-tuple-element.65), channel_id=1, source_target_pairs={{0,24},{1,25},{2,26},{3,27},{4,28},{5,29},{6,30},{7,31},{8,0},{9,1... | collective-permute-start | bytes 294920 | tf_op jit(solution)/shard_map/ppermute | solution.py:284
  52.8 5.0 %collective-permute-start.8 = (bf16[2,48,512]{2,1,0:T(8,128)(2,1)S(1)}, bf16[2,48,512]{2,1,0:T(8,128)(2,1)S(1)}, u32[]{:S(2)}, u32[]{:S(2)}) collective-permute-start(bf16[2,48,512]{2,1,0:T(8,128)(2,1)S(1)} %get-tuple-element.67), channel_id=1, source_target_pairs={{0,8},{1,9},{2,10},{3,11},{4,12},{5,13},{6,14},{7,15},{8,16},{9,17... | collective-permute-start | bytes 294920 | tf_op jit(solution)/shard_map/ppermute | solution.py:284
  54.2 5.0 %collective-permute-start.9 = (bf16[2,48,512]{2,1,0:T(8,128)(2,1)S(1)}, bf16[2,48,512]{2,1,0:T(8,128)(2,1)S(1)}, u32[]{:S(2)}, u32[]{:S(2)}) collective-permute-start(bf16[2,48,512]{2,1,0:T(8,128)(2,1)S(1)} %get-tuple-element.66), channel_id=1, source_target_pairs={{0,16},{1,17},{2,18},{3,19},{4,20},{5,21},{6,22},{7,23},{8,24},{9,... | collective-permute-start | bytes 294920 | tf_op jit(solution)/shard_map/ppermute | solution.py:284
  59.6 11.5 %collective-permute-start.12 = (bf16[4,48,512]{2,1,0:T(8,128)(2,1)S(1)}, bf16[4,48,512]{2,1,0:T(8,128)(2,1)S(1)}, u32[]{:S(2)}, u32[]{:S(2)}) collective-permute-start(bf16[4,48,512]{2,1,0:T(8,128)(2,1)S(1)} %fusion), channel_id=1, source_target_pairs={{0,96},{32,0},{64,32},{96,64},{1,97},{33,1},{65,33},{97,65},{2,98}... | collective-permute-start | bytes 589832 | tf_op jit(solution)/shard_map/ppermute | solution.py:281
  62.1 9.0 %collective-permute-start.11 = (bf16[4,48,512]{2,1,0:T(8,128)(2,1)S(1)}, bf16[4,48,512]{2,1,0:T(8,128)(2,1)S(1)}, u32[]{:S(2)}, u32[]{:S(2)}) collective-permute-start(bf16[4,48,512]{2,1,0:T(8,128)(2,1)S(1)} %fusion.1), channel_id=1, source_target_pairs={{0,32},{32,64},{64,96},{96,0},{1,33},{33,65},{65,97},{97,1},{2,34}... | collective-permute-start | bytes 589832 | tf_op jit(solution)/shard_map/ppermute | solution.py:281
  62.2 7.4 %collective-permute-start.13 = (bf16[2,48,512]{2,1,0:T(8,128)(2,1)S(1)}, bf16[2,48,512]{2,1,0:T(8,128)(2,1)S(1)}, u32[]{:S(2)}, u32[]{:S(2)}) collective-permute-start(bf16[2,48,512]{2,1,0:T(8,128)(2,1)S(1)} %get-tuple-element.81), channel_id=1, source_target_pairs={{0,32},{32,64},{64,96},{96,0},{1,33},{33,65},{65,97},{97,1},{2,34}... | collective-permute-start | bytes 294920 | tf_op jit(solution)/shard_map/ppermute | solution.py:281
  62.3 8.0 %collective-permute-start.14 = (bf16[2,48,512]{2,1,0:T(8,128)(2,1)S(1)}, bf16[2,48,512]{2,1,0:T(8,128)(2,1)S(1)}, u32[]{:S(2)}, u32[]{:S(2)}) collective-permute-start(bf16[2,48,512]{2,1,0:T(8,128)(2,1)S(1)} %get-tuple-element.80), channel_id=1, source_target_pairs={{0,64},{32,96},{64,0},{96,32},{1,65},{33,97},{65,1},{97,33},{2,66}... | collective-permute-start | bytes 294920 | tf_op jit(solution)/shard_map/ppermute | solution.py:281
  66.1 4.9 %collective-permute-start.15 = (bf16[2,48,512]{2,1,0:T(8,128)(2,1)S(1)}, bf16[2,48,512]{2,1,0:T(8,128)(2,1)S(1)}, u32[]{:S(2)}, u32[]{:S(2)}) collective-permute-start(bf16[2,48,512]{2,1,0:T(8,128)(2,1)S(1)} %get-tuple-element.79), channel_id=1, source_target_pairs={{0,96},{32,0},{64,32},{96,64},{1,97},{33,1},{65,33},{97,65},{2,98}... | collective-permute-start | bytes 294920 | tf_op jit(solution)/shard_map/ppermute | solution.py:281
  71.3 4.6 %collective-permute-start.18 = (bf16[2,2,48,512]{3,2,0,1:T(8,128)(2,1)S(1)}, bf16[2,2,48,512]{3,2,0,1:T(8,128)(2,1)S(1)}, u32[]{:S(2)}, u32[]{:S(2)}) collective-permute-start(bf16[2,2,48,512]{3,2,0,1:T(8,128)(2,1)S(1)} %pad_maximum_fusion.4), channel_id=1, source_target_pairs={{0,6},{1,7},{2,0},{3,1},{4,2},{5,3},{6,4},{7,5},{8,14},{9,15},{10,... | collective-permute-start | bytes 589832 | tf_op jit(solution)/shard_map/ppermute | solution.py:284
  72.1 6.1 %collective-permute-start.17 = (bf16[2,2,48,512]{3,2,1,0:T(8,128)(2,1)S(1)}, bf16[2,2,48,512]{3,2,1,0:T(8,128)(2,1)S(1)}, u32[]{:S(2)}, u32[]{:S(2)}) collective-permute-start(bf16[2,2,48,512]{3,2,1,0:T(8,128)(2,1)S(1)} %pad_maximum_fusion.3), channel_id=1, source_target_pairs={{0,4},{1,5},{2,6},{3,7},{4,0},{5,1},{6,2},{7,3},{8,12},{9,13},{10,... | collective-permute-start | bytes 589832 | tf_op jit(solution)/shard_map/ppermute | solution.py:284
  74.2 6.1 %collective-permute-start.16 = (bf16[2,2,48,512]{3,2,1,0:T(8,128)(2,1)S(1)}, bf16[2,2,48,512]{3,2,1,0:T(8,128)(2,1)S(1)}, u32[]{:S(2)}, u32[]{:S(2)}) collective-permute-start(bf16[2,2,48,512]{3,2,1,0:T(8,128)(2,1)S(1)} %pad_maximum_fusion.2), channel_id=1, source_target_pairs={{0,2},{1,3},{2,4},{3,5},{4,6},{5,7},{6,0},{7,1},{8,10},{9,11},{10,... | collective-permute-start | bytes 589832 | tf_op jit(solution)/shard_map/ppermute | solution.py:284
  80.4 8.0 %collective-permute-start.19 = (bf16[4,2,48,512]{3,2,1,0:T(8,128)(2,1)S(1)}, bf16[4,2,48,512]{3,2,1,0:T(8,128)(2,1)S(1)}, u32[]{:S(2)}, u32[]{:S(2)}) collective-permute-start(bf16[4,2,48,512]{3,2,1,0:T(8,128)(2,1)S(1)} %pad_maximum_fusion), channel_id=1, source_target_pairs={{0,1},{1,0},{2,3},{3,2},{4,5},{5,4},{6,7},{7,6},{8,9},{9,8},{10,11... | collective-permute-start | bytes 1179656 | tf_op jit(solution)/shard_map/ppermute | solution.py:284

commit v4 on v3

--- a/solution.py
+++ b/solution.py
@@ -11,7 +11,7 @@
 ROOM = 64
 LINE, CORES, TEAM, RING = 4, 2, 8, 4
 VMEM = 28 * 2**20
-ALL_VMEM = 58 * 2**20
+ALL_VMEM = 28 * 2**20
 
 f32, bf16, i32 = jnp.float32, jnp.bfloat16, jnp.int32
 ANY = pl.BlockSpec(memory_space=pl.ANY)
@@ -146,8 +146,6 @@
     def merge(level):
         counts, uses = lists[2 * level:2 * level + 2]
         for k in range(kinds):
-            if level == 0:
-                mat_copies[k].wait()
             multiply(level, k, [uses[k * ROOM + i] for i in range(TAKE)])
 
         def rest(k, carry):
@@ -175,14 +173,17 @@
                 stage[place] = merged
 
     index_copy.wait()
-    sort_level(0)
+    for level in range(levels if joined else 1):
+        sort_level(level)
     for copy in feeds:
         copy.wait()
     if not joined:
         for o in range(images):
             image[0, o] = projected(o, foot, weights, rows)
+    for copy in mat_copies:
+        copy.wait()
     for level in range(levels):
-        if level + 1 < levels:
+        if level + 1 < levels and not joined:
             sort_level(level + 1)
         merge(level)
 

time: 89.6 us -> 88.4 us (0.987)
  Pallas kernels: 39.6 us -> 36.9 us
    pallas_call x2, Pallas kernels: 33.2 us -> 30.2 us  [trees(): pl.pallas_call(functools.partial(tree_kernel, joined, block, levels), in_...]
  transfers between devices with their start and end apart: 20 -> 20, of which waited for: 11 -> 11; matrix products, arithmetic and copies ran while one was open for 0% -> 0% of each run, Pallas kernels for 37% -> 34%
where the time goes in v4:
time: 88.4 us; the launch traced here: 88 us
  Pallas kernels  36.9 us (42%)
  starting transfers between devices  32.3 us (37%)
  waiting for transfers between devices  17.6 us (20%)
    pallas_call x2, Pallas kernels, trees(): pl.pallas_call(functools.partial(tree_kernel, joined, block, levels), in_...  30.2 us
    ppermute x10, starting transfers between devices, along_sub(): lax.ppermute(value, 'sub', [(i, move(i >> 3, i >> 1 & 3, i & 1)) for i in...  18.1 us
    ppermute x10, starting transfers between devices, along_y(): lax.ppermute(value, 'grp', [(i, (i + d) % RING) for i in range(RING)])  14.2 us
    ppermute x10, waiting for transfers between devices, along_sub(): lax.ppermute(value, 'sub', [(i, move(i >> 3, i >> 1 & 3, i & 1)) for i in...  12.3 us
    pallas_call x1, Pallas kernels, start_images(): pl.pallas_call(functools.partial(start_kernel, block), in_specs=[HBM] * 3...  5.48 us
    ppermute x10, waiting for transfers between devices, along_y(): lax.ppermute(value, 'grp', [(i, (i + d) % RING) for i in range(RING)])  5.29 us
  transfers between devices with their start and end apart: 20, of which 11 were waited for; matrix products, arithmetic and copies ran while one was open for 0% of the time, Pallas kernels for 34%

profile of v4, /device:TPU:1, one launch (start us, length us, event | category | flops | bytes accessed | tf_op | source)
XLA Modules:
  0.0 88.0 jit_solution(11757659634938317954)
XLA Ops:
  0.0 5.5 %start.1 = (bf16[8,48,512]{2,1,0:T(8,128)(2,1)S(1)}, bf16[8,48,512]{2,1,0:T(8,128)(2,1)S(1)}, bf16[8,48,512]{2,1,0:T(8,128)(2,1)S(1)}, bf16[8,48,512]{2,1,0:T(8,128)(2,1)S(1)}) custom-call(s32[2,32]{1,0:T(2,128)} %bitcast.55, bf16[32,128,1024]{2,1,0:T(8,128)(2,1)} %bitcast.53, bf16[32,48,256]{2,1,0:T(8,128)(2,1)} %refs_2_.1), custom_call_target="tpu_custom_call" | custom-call | flops 400000000 | bytes 7340032 | tf_op jit(solution)/shard_map/start/pallas_call | solution.py:65
  5.5 2.5 %collective-permute-start.3 = (bf16[8,48,512]{2,1,0:T(8,128)(2,1)S(1)}, bf16[8,48,512]{2,1,0:T(8,128)(2,1)S(1)}, u32[]{:S(2)}, u32[]{:S(2)}) collective-permute-start(bf16[8,48,512]{2,1,0:T(8,128)(2,1)S(1)} %get-tuple-element.40), channel_id=1, source_target_pairs={{0,8},{1,9},{2,10},{3,11},{4,12},{5,13},{6,14},{7,15},{8,16},{9,17... | collective-permute-start | bytes 1179656 | tf_op jit(solution)/shard_map/ppermute | solution.py:285
  8.0 3.3 %collective-permute-start.4 = (bf16[8,48,512]{2,1,0:T(8,128)(2,1)S(1)}, bf16[8,48,512]{2,1,0:T(8,128)(2,1)S(1)}, u32[]{:S(2)}, u32[]{:S(2)}) collective-permute-start(bf16[8,48,512]{2,1,0:T(8,128)(2,1)S(1)} %get-tuple-element.41), channel_id=1, source_target_pairs={{0,16},{1,17},{2,18},{3,19},{4,20},{5,21},{6,22},{7,23},{8,24},{9,... | collective-permute-start | bytes 1179656 | tf_op jit(solution)/shard_map/ppermute | solution.py:285
  12.1 15.7 %trees.1 = (bf16[8,48,512]{2,1,0:T(8,128)(2,1)S(1)}, bf16[8,48,512]{2,1,0:T(8,128)(2,1)S(1)}, bf16[8,48,512]{2,1,0:T(8,128)(2,1)S(1)}, bf16[8,48,512]{2,1,0:T(8,128)(2,1)S(1)}) custom-call(s32[2,32]{1,0:T(2,128)} %bitcast.56, bf16[32,128,1024]{2,1,0:T(8,128)(2,1)} %bitcast.54, bf16[32,48,256]{2,1,0:T(8,128)(2,1)} %refs_2_.1, ...), custom_call_target="tpu_custom_call" | custom-call | flops 8999999488 | bytes 11534336 | tf_op jit(solution)/shard_map/trees/pallas_call | solution.py:232
  27.7 1.6 %collective-permute-start = (bf16[8,48,512]{2,1,0:T(8,128)(2,1)S(1)}, bf16[8,48,512]{2,1,0:T(8,128)(2,1)S(1)}, u32[]{:S(2)}, u32[]{:S(2)}) collective-permute-start(bf16[8,48,512]{2,1,0:T(8,128)(2,1)S(1)} %get-tuple-element.37), channel_id=1, source_target_pairs={{0,32},{32,64},{64,96},{96,0},{1,33},{33,65},{65,97},{97,1},{2,34}... | collective-permute-start | bytes 1179656 | tf_op jit(solution)/shard_map/ppermute | solution.py:282
  29.4 2.1 %collective-permute-start.1 = (bf16[8,48,512]{2,1,0:T(8,128)(2,1)S(1)}, bf16[8,48,512]{2,1,0:T(8,128)(2,1)S(1)}, u32[]{:S(2)}, u32[]{:S(2)}) collective-permute-start(bf16[8,48,512]{2,1,0:T(8,128)(2,1)S(1)} %get-tuple-element.38), channel_id=1, source_target_pairs={{0,64},{32,96},{64,0},{96,32},{1,65},{33,97},{65,1},{97,33},{2,66}... | collective-permute-start | bytes 1179656 | tf_op jit(solution)/shard_map/ppermute | solution.py:282
  31.5 1.3 %collective-permute-start.2 = (bf16[8,48,512]{2,1,0:T(8,128)(2,1)S(1)}, bf16[8,48,512]{2,1,0:T(8,128)(2,1)S(1)}, u32[]{:S(2)}, u32[]{:S(2)}) collective-permute-start(bf16[8,48,512]{2,1,0:T(8,128)(2,1)S(1)} %get-tuple-element.39), channel_id=1, source_target_pairs={{0,96},{32,0},{64,32},{96,64},{1,97},{33,1},{65,33},{97,65},{2,98}... | collective-permute-start | bytes 1179656 | tf_op jit(solution)/shard_map/ppermute | solution.py:282
  32.8 14.5 %joined_trees.1 = (bf16[2,4,48,512]{3,2,1,0:T(8,128)(2,1)S(1)}, bf16[2,4,48,512]{3,2,1,0:T(8,128)(2,1)S(1)}, bf16[4,48,512]{2,1,0:T(8,128)(2,1)S(1)}, bf16[4,48,...) custom-call(bf16[8,48,512]{2,1,0:T(8,128)(2,1)S(1)} %get-tuple-element.35.refs_3_.refs_0_, ...), custom_call_target="tpu_custom_call" | custom-call | flops 8999999488 | bytes 11534336 | tf_op jit(solution)/shard_map/joined_trees/pallas_call | solution.py:232
  48.1 2.0 %collective-permute-start.7 = (bf16[2,4,48,512]{3,2,1,0:T(8,128)(2,1)S(1)}, bf16[2,4,48,512]{3,2,1,0:T(8,128)(2,1)S(1)}, u32[]{:S(2)}, u32[]{:S(2)}) collective-permute-start(bf16[2,4,48,512]{3,2,1,0:T(8,128)(2,1)S(1)} %get-tuple-element.46), channel_id=1, source_target_pairs={{0,96},{32,0},{64,32},{96,64},{1,97},{33,1},{65,33},{97,65},{2,98}... | collective-permute-start | bytes 1179656 | tf_op jit(solution)/shard_map/ppermute | solution.py:282
  50.4 1.5 %collective-permute-start.8 = (bf16[2,48,512]{2,1,0:T(8,128)(2,1)S(1)}, bf16[2,48,512]{2,1,0:T(8,128)(2,1)S(1)}, u32[]{:S(2)}, u32[]{:S(2)}) collective-permute-start(bf16[2,48,512]{2,1,0:T(8,128)(2,1)S(1)} %get-tuple-element.67), channel_id=1, source_target_pairs={{0,8},{1,9},{2,10},{3,11},{4,12},{5,13},{6,14},{7,15},{8,16},{9,17... | collective-permute-start | bytes 294920 | tf_op jit(solution)/shard_map/ppermute | solution.py:285
  52.7 1.5 %collective-permute-done.10 = bf16[2,48,512]{2,1,0:T(8,128)(2,1)S(1)} collective-permute-done((bf16[2,48,512]{2,1,0:T(8,128)(2,1)S(1)}, bf16[2,48,512]{2,1,0:T(8,128)(2,1)S(1)}, u32[]{:S(2)}, u32[]{:S(2)}) %collective-permute-start.10) | collective-permute-done | bytes 98336 | tf_op jit(solution)/shard_map/ppermute | solution.py:285
  54.2 1.3 %collective-permute-done.8 = bf16[2,48,512]{2,1,0:T(8,128)(2,1)S(1)} collective-permute-done((bf16[2,48,512]{2,1,0:T(8,128)(2,1)S(1)}, bf16[2,48,512]{2,1,0:T(8,128)(2,1)S(1)}, u32[]{:S(2)}, u32[]{:S(2)}) %collective-permute-start.8) | collective-permute-done | bytes 98336 | tf_op jit(solution)/shard_map/ppermute | solution.py:285
  55.5 1.4 %collective-permute-done.9 = bf16[2,48,512]{2,1,0:T(8,128)(2,1)S(1)} collective-permute-done((bf16[2,48,512]{2,1,0:T(8,128)(2,1)S(1)}, bf16[2,48,512]{2,1,0:T(8,128)(2,1)S(1)}, u32[]{:S(2)}, u32[]{:S(2)}) %collective-permute-start.9) | collective-permute-done | bytes 98336 | tf_op jit(solution)/shard_map/ppermute | solution.py:285
  57.5 2.5 %collective-permute-start.12 = (bf16[4,48,512]{2,1,0:T(8,128)(2,1)S(1)}, bf16[4,48,512]{2,1,0:T(8,128)(2,1)S(1)}, u32[]{:S(2)}, u32[]{:S(2)}) collective-permute-start(bf16[4,48,512]{2,1,0:T(8,128)(2,1)S(1)} %fusion), channel_id=1, source_target_pairs={{0,96},{32,0},{64,32},{96,64},{1,97},{33,1},{65,33},{97,65},{2,98}... | collective-permute-start | bytes 589832 | tf_op jit(solution)/shard_map/ppermute | solution.py:282
  60.2 3.8 %collective-permute-start.14 = (bf16[2,48,512]{2,1,0:T(8,128)(2,1)S(1)}, bf16[2,48,512]{2,1,0:T(8,128)(2,1)S(1)}, u32[]{:S(2)}, u32[]{:S(2)}) collective-permute-start(bf16[2,48,512]{2,1,0:T(8,128)(2,1)S(1)} %get-tuple-element.80), channel_id=1, source_target_pairs={{0,64},{32,96},{64,0},{96,32},{1,65},{33,97},{65,1},{97,33},{2,66}... | collective-permute-start | bytes 294920 | tf_op jit(solution)/shard_map/ppermute | solution.py:282
  64.0 3.2 %collective-permute-done.13 = bf16[2,48,512]{2,1,0:T(8,128)(2,1)S(1)} collective-permute-done((bf16[2,48,512]{2,1,0:T(8,128)(2,1)S(1)}, bf16[2,48,512]{2,1,0:T(8,128)(2,1)S(1)}, u32[]{:S(2)}, u32[]{:S(2)}) %collective-permute-start.13) | collective-permute-done | bytes 98336 | tf_op jit(solution)/shard_map/ppermute | solution.py:282
  67.3 1.2 %collective-permute-done.14 = bf16[2,48,512]{2,1,0:T(8,128)(2,1)S(1)} collective-permute-done((bf16[2,48,512]{2,1,0:T(8,128)(2,1)S(1)}, bf16[2,48,512]{2,1,0:T(8,128)(2,1)S(1)}, u32[]{:S(2)}, u32[]{:S(2)}) %collective-permute-start.14) | collective-permute-done | bytes 98336 | tf_op jit(solution)/shard_map/ppermute | solution.py:282
  69.0 2.1 %collective-permute-start.18 = (bf16[2,2,48,512]{3,2,0,1:T(8,128)(2,1)S(1)}, bf16[2,2,48,512]{3,2,0,1:T(8,128)(2,1)S(1)}, u32[]{:S(2)}, u32[]{:S(2)}) collective-permute-start(bf16[2,2,48,512]{3,2,0,1:T(8,128)(2,1)S(1)} %pad_maximum_fusion.4), channel_id=1, source_target_pairs={{0,6},{1,7},{2,0},{3,1},{4,2},{5,3},{6,4},{7,5},{8,14},{9,15},{10,... | collective-permute-start | bytes 589832 | tf_op jit(solution)/shard_map/ppermute | solution.py:285
  72.5 3.3 %collective-permute-done.18 = bf16[2,2,48,512]{3,2,0,1:T(8,128)(2,1)S(1)} collective-permute-done((bf16[2,2,48,512]{3,2,0,1:T(8,128)(2,1)S(1)}, bf16[2,2,48,512]{3,2,0,1:T(8,128)(2,1)S(1)}, u32[]{:S(2)}, u32[]{:S(2)}) %collective-permute-start.18) | collective-permute-done | bytes 196640 | tf_op jit(solution)/shard_map/ppermute | solution.py:285
  75.8 1.5 %collective-permute-done.17.refs_2_ = bf16[2,2,48,512]{3,2,1,0:T(8,128)(2,1)S(1)} collective-permute-done((bf16[2,2,48,512]{3,2,1,0:T(8,128)(2,1)S(1)}, bf16[2,2,48,512]{3,2,1,0:T(8,128)(2,1)S(1)}, u32[]{:S(2)}, u32[]{:S(2)}) %collective-permute-start.17) | collective-permute-done | bytes 196640 | tf_op jit(solution)/shard_map/ppermute | solution.py:285
  77.4 2.0 %collective-permute-done.16.refs_1_ = bf16[2,2,48,512]{3,2,1,0:T(8,128)(2,1)S(1)} collective-permute-done((bf16[2,2,48,512]{3,2,1,0:T(8,128)(2,1)S(1)}, bf16[2,2,48,512]{3,2,1,0:T(8,128)(2,1)S(1)}, u32[]{:S(2)}, u32[]{:S(2)}) %collective-permute-start.16) | collective-permute-done | bytes 196640 | tf_op jit(solution)/shard_map/ppermute | solution.py:285
  79.4 5.8 %collective-permute-start.19 = (bf16[4,2,48,512]{3,2,1,0:T(8,128)(2,1)S(1)}, bf16[4,2,48,512]{3,2,1,0:T(8,128)(2,1)S(1)}, u32[]{:S(2)}, u32[]{:S(2)}) collective-permute-start(bf16[4,2,48,512]{3,2,1,0:T(8,128)(2,1)S(1)} %pad_maximum_fusion), channel_id=1, source_target_pairs={{0,1},{1,0},{2,3},{3,2},{4,5},{5,4},{6,7},{7,6},{8,9},{9,8},{10,11... | collective-permute-start | bytes 1179656 | tf_op jit(solution)/shard_map/ppermute | solution.py:285
  85.3 1.3 %collective-permute-done.19.refs_4_ = bf16[4,2,48,512]{3,2,1,0:T(8,128)(2,1)S(1)} collective-permute-done((bf16[4,2,48,512]{3,2,1,0:T(8,128)(2,1)S(1)}, bf16[4,2,48,512]{3,2,1,0:T(8,128)(2,1)S(1)}, u32[]{:S(2)}, u32[]{:S(2)}) %collective-permute-start.19) | collective-permute-done | bytes 393248 | tf_op jit(solution)/shard_map/ppermute | solution.py:285
  86.6 1.2 %lay.1 = bf16[48,8192]{1,0:T(8,128)(2,1)} custom-call(bf16[2,2,48,512]{3,2,1,0:T(8,128)(2,1)S(1)} %pad_maximum_fusion.1.refs_0_, bf16[2,2,48,512]{3,2,1,0:T(8,128)(2,1)S(1)} %collective-permute-done.16.refs_1_, bf16[2,2,48,512]{3,2,1,0:T(8,128)(2,1)S(1)} %collective-permute-done.17.refs_2_, bf16[2,2,48,512]{3,2,1,0:T(8,128)(2,1)S(1)} %copy.8.refs_3_, ...), custom_call_target="tpu_custom_call" | custom-call | tf_op jit(solution)/shard_map/lay/pallas_call | solution.py:323
  (36 shorter events, 5.4 us)
Async XLA Ops:
  5.5 26.0 %collective-permute-start.3 = (bf16[8,48,512]{2,1,0:T(8,128)(2,1)S(1)}, bf16[8,48,512]{2,1,0:T(8,128)(2,1)S(1)}, u32[]{:S(2)}, u32[]{:S(2)}) collective-permute-start(bf16[8,48,512]{2,1,0:T(8,128)(2,1)S(1)} %get-tuple-element.40), channel_id=1, source_target_pairs={{0,8},{1,9},{2,10},{3,11},{4,12},{5,13},{6,14},{7,15},{8,16},{9,17... | collective-permute-start | bytes 1179656 | tf_op jit(solution)/shard_map/ppermute | solution.py:285
  8.0 24.8 %collective-permute-start.4 = (bf16[8,48,512]{2,1,0:T(8,128)(2,1)S(1)}, bf16[8,48,512]{2,1,0:T(8,128)(2,1)S(1)}, u32[]{:S(2)}, u32[]{:S(2)}) collective-permute-start(bf16[8,48,512]{2,1,0:T(8,128)(2,1)S(1)} %get-tuple-element.41), channel_id=1, source_target_pairs={{0,16},{1,17},{2,18},{3,19},{4,20},{5,21},{6,22},{7,23},{8,24},{9,... | collective-permute-start | bytes 1179656 | tf_op jit(solution)/shard_map/ppermute | solution.py:285
  11.3 21.5 %collective-permute-start.5 = (bf16[8,48,512]{2,1,0:T(8,128)(2,1)S(1)}, bf16[8,48,512]{2,1,0:T(8,128)(2,1)S(1)}, u32[]{:S(2)}, u32[]{:S(2)}) collective-permute-start(bf16[8,48,512]{2,1,0:T(8,128)(2,1)S(1)} %get-tuple-element.42), channel_id=1, source_target_pairs={{0,24},{1,25},{2,26},{3,27},{4,28},{5,29},{6,30},{7,31},{8,0},{9,1... | collective-permute-start | bytes 1179656 | tf_op jit(solution)/shard_map/ppermute | solution.py:285
  27.7 22.4 %collective-permute-start = (bf16[8,48,512]{2,1,0:T(8,128)(2,1)S(1)}, bf16[8,48,512]{2,1,0:T(8,128)(2,1)S(1)}, u32[]{:S(2)}, u32[]{:S(2)}) collective-permute-start(bf16[8,48,512]{2,1,0:T(8,128)(2,1)S(1)} %get-tuple-element.37), channel_id=1, source_target_pairs={{0,32},{32,64},{64,96},{96,0},{1,33},{33,65},{65,97},{97,1},{2,34}... | collective-permute-start | bytes 1179656 | tf_op jit(solution)/shard_map/ppermute | solution.py:282
  29.4 20.7 %collective-permute-start.1 = (bf16[8,48,512]{2,1,0:T(8,128)(2,1)S(1)}, bf16[8,48,512]{2,1,0:T(8,128)(2,1)S(1)}, u32[]{:S(2)}, u32[]{:S(2)}) collective-permute-start(bf16[8,48,512]{2,1,0:T(8,128)(2,1)S(1)} %get-tuple-element.38), channel_id=1, source_target_pairs={{0,64},{32,96},{64,0},{96,32},{1,65},{33,97},{65,1},{97,33},{2,66}... | collective-permute-start | bytes 1179656 | tf_op jit(solution)/shard_map/ppermute | solution.py:282
  31.5 18.6 %collective-permute-start.2 = (bf16[8,48,512]{2,1,0:T(8,128)(2,1)S(1)}, bf16[8,48,512]{2,1,0:T(8,128)(2,1)S(1)}, u32[]{:S(2)}, u32[]{:S(2)}) collective-permute-start(bf16[8,48,512]{2,1,0:T(8,128)(2,1)S(1)} %get-tuple-element.39), channel_id=1, source_target_pairs={{0,96},{32,0},{64,32},{96,64},{1,97},{33,1},{65,33},{97,65},{2,98}... | collective-permute-start | bytes 1179656 | tf_op jit(solution)/shard_map/ppermute | solution.py:282
  47.4 10.0 %collective-permute-start.6 = (bf16[2,4,48,512]{3,2,1,0:T(8,128)(2,1)S(1)}, bf16[2,4,48,512]{3,2,1,0:T(8,128)(2,1)S(1)}, u32[]{:S(2)}, u32[]{:S(2)}) collective-permute-start(bf16[2,4,48,512]{3,2,1,0:T(8,128)(2,1)S(1)} %get-tuple-element.45), channel_id=1, source_target_pairs={{0,32},{32,64},{64,96},{96,0},{1,33},{33,65},{65,97},{97,1},{2,34}... | collective-permute-start | bytes 1179656 | tf_op jit(solution)/shard_map/ppermute | solution.py:282
  48.1 9.3 %collective-permute-start.7 = (bf16[2,4,48,512]{3,2,1,0:T(8,128)(2,1)S(1)}, bf16[2,4,48,512]{3,2,1,0:T(8,128)(2,1)S(1)}, u32[]{:S(2)}, u32[]{:S(2)}) collective-permute-start(bf16[2,4,48,512]{3,2,1,0:T(8,128)(2,1)S(1)} %get-tuple-element.46), channel_id=1, source_target_pairs={{0,96},{32,0},{64,32},{96,64},{1,97},{33,1},{65,33},{97,65},{2,98}... | collective-permute-start | bytes 1179656 | tf_op jit(solution)/shard_map/ppermute | solution.py:282
  50.3 3.8 %collective-permute-start.10 = (bf16[2,48,512]{2,1,0:T(8,128)(2,1)S(1)}, bf16[2,48,512]{2,1,0:T(8,128)(2,1)S(1)}, u32[]{:S(2)}, u32[]{:S(2)}) collective-permute-start(bf16[2,48,512]{2,1,0:T(8,128)(2,1)S(1)} %get-tuple-element.65), channel_id=1, source_target_pairs={{0,24},{1,25},{2,26},{3,27},{4,28},{5,29},{6,30},{7,31},{8,0},{9,1... | collective-permute-start | bytes 294920 | tf_op jit(solution)/shard_map/ppermute | solution.py:285
  50.4 5.0 %collective-permute-start.8 = (bf16[2,48,512]{2,1,0:T(8,128)(2,1)S(1)}, bf16[2,48,512]{2,1,0:T(8,128)(2,1)S(1)}, u32[]{:S(2)}, u32[]{:S(2)}) collective-permute-start(bf16[2,48,512]{2,1,0:T(8,128)(2,1)S(1)} %get-tuple-element.67), channel_id=1, source_target_pairs={{0,8},{1,9},{2,10},{3,11},{4,12},{5,13},{6,14},{7,15},{8,16},{9,17... | collective-permute-start | bytes 294920 | tf_op jit(solution)/shard_map/ppermute | solution.py:285
  51.9 5.0 %collective-permute-start.9 = (bf16[2,48,512]{2,1,0:T(8,128)(2,1)S(1)}, bf16[2,48,512]{2,1,0:T(8,128)(2,1)S(1)}, u32[]{:S(2)}, u32[]{:S(2)}) collective-permute-start(bf16[2,48,512]{2,1,0:T(8,128)(2,1)S(1)} %get-tuple-element.66), channel_id=1, source_target_pairs={{0,16},{1,17},{2,18},{3,19},{4,20},{5,21},{6,22},{7,23},{8,24},{9,... | collective-permute-start | bytes 294920 | tf_op jit(solution)/shard_map/ppermute | solution.py:285
  57.5 11.3 %collective-permute-start.12 = (bf16[4,48,512]{2,1,0:T(8,128)(2,1)S(1)}, bf16[4,48,512]{2,1,0:T(8,128)(2,1)S(1)}, u32[]{:S(2)}, u32[]{:S(2)}) collective-permute-start(bf16[4,48,512]{2,1,0:T(8,128)(2,1)S(1)} %fusion), channel_id=1, source_target_pairs={{0,96},{32,0},{64,32},{96,64},{1,97},{33,1},{65,33},{97,65},{2,98}... | collective-permute-start | bytes 589832 | tf_op jit(solution)/shard_map/ppermute | solution.py:282
  60.0 8.8 %collective-permute-start.11 = (bf16[4,48,512]{2,1,0:T(8,128)(2,1)S(1)}, bf16[4,48,512]{2,1,0:T(8,128)(2,1)S(1)}, u32[]{:S(2)}, u32[]{:S(2)}) collective-permute-start(bf16[4,48,512]{2,1,0:T(8,128)(2,1)S(1)} %fusion.1), channel_id=1, source_target_pairs={{0,32},{32,64},{64,96},{96,0},{1,33},{33,65},{65,97},{97,1},{2,34}... | collective-permute-start | bytes 589832 | tf_op jit(solution)/shard_map/ppermute | solution.py:282
  60.1 7.1 %collective-permute-start.13 = (bf16[2,48,512]{2,1,0:T(8,128)(2,1)S(1)}, bf16[2,48,512]{2,1,0:T(8,128)(2,1)S(1)}, u32[]{:S(2)}, u32[]{:S(2)}) collective-permute-start(bf16[2,48,512]{2,1,0:T(8,128)(2,1)S(1)} %get-tuple-element.81), channel_id=1, source_target_pairs={{0,32},{32,64},{64,96},{96,0},{1,33},{33,65},{65,97},{97,1},{2,34}... | collective-permute-start | bytes 294920 | tf_op jit(solution)/shard_map/ppermute | solution.py:282
  60.2 8.3 %collective-permute-start.14 = (bf16[2,48,512]{2,1,0:T(8,128)(2,1)S(1)}, bf16[2,48,512]{2,1,0:T(8,128)(2,1)S(1)}, u32[]{:S(2)}, u32[]{:S(2)}) collective-permute-start(bf16[2,48,512]{2,1,0:T(8,128)(2,1)S(1)} %get-tuple-element.80), channel_id=1, source_target_pairs={{0,64},{32,96},{64,0},{96,32},{1,65},{33,97},{65,1},{97,33},{2,66}... | collective-permute-start | bytes 294920 | tf_op jit(solution)/shard_map/ppermute | solution.py:282
  64.0 4.7 %collective-permute-start.15 = (bf16[2,48,512]{2,1,0:T(8,128)(2,1)S(1)}, bf16[2,48,512]{2,1,0:T(8,128)(2,1)S(1)}, u32[]{:S(2)}, u32[]{:S(2)}) collective-permute-start(bf16[2,48,512]{2,1,0:T(8,128)(2,1)S(1)} %get-tuple-element.79), channel_id=1, source_target_pairs={{0,96},{32,0},{64,32},{96,64},{1,97},{33,1},{65,33},{97,65},{2,98}... | collective-permute-start | bytes 294920 | tf_op jit(solution)/shard_map/ppermute | solution.py:282
  69.0 6.8 %collective-permute-start.18 = (bf16[2,2,48,512]{3,2,0,1:T(8,128)(2,1)S(1)}, bf16[2,2,48,512]{3,2,0,1:T(8,128)(2,1)S(1)}, u32[]{:S(2)}, u32[]{:S(2)}) collective-permute-start(bf16[2,2,48,512]{3,2,0,1:T(8,128)(2,1)S(1)} %pad_maximum_fusion.4), channel_id=1, source_target_pairs={{0,6},{1,7},{2,0},{3,1},{4,2},{5,3},{6,4},{7,5},{8,14},{9,15},{10,... | collective-permute-start | bytes 589832 | tf_op jit(solution)/shard_map/ppermute | solution.py:285
  71.1 6.2 %collective-permute-start.17 = (bf16[2,2,48,512]{3,2,1,0:T(8,128)(2,1)S(1)}, bf16[2,2,48,512]{3,2,1,0:T(8,128)(2,1)S(1)}, u32[]{:S(2)}, u32[]{:S(2)}) collective-permute-start(bf16[2,2,48,512]{3,2,1,0:T(8,128)(2,1)S(1)} %pad_maximum_fusion.3), channel_id=1, source_target_pairs={{0,4},{1,5},{2,6},{3,7},{4,0},{5,1},{6,2},{7,3},{8,12},{9,13},{10,... | collective-permute-start | bytes 589832 | tf_op jit(solution)/shard_map/ppermute | solution.py:285
  71.6 7.8 %collective-permute-start.16 = (bf16[2,2,48,512]{3,2,1,0:T(8,128)(2,1)S(1)}, bf16[2,2,48,512]{3,2,1,0:T(8,128)(2,1)S(1)}, u32[]{:S(2)}, u32[]{:S(2)}) collective-permute-start(bf16[2,2,48,512]{3,2,1,0:T(8,128)(2,1)S(1)} %pad_maximum_fusion.2), channel_id=1, source_target_pairs={{0,2},{1,3},{2,4},{3,5},{4,6},{5,7},{6,0},{7,1},{8,10},{9,11},{10,... | collective-permute-start | bytes 589832 | tf_op jit(solution)/shard_map/ppermute | solution.py:285
  79.4 7.2 %collective-permute-start.19 = (bf16[4,2,48,512]{3,2,1,0:T(8,128)(2,1)S(1)}, bf16[4,2,48,512]{3,2,1,0:T(8,128)(2,1)S(1)}, u32[]{:S(2)}, u32[]{:S(2)}) collective-permute-start(bf16[4,2,48,512]{3,2,1,0:T(8,128)(2,1)S(1)} %pad_maximum_fusion), channel_id=1, source_target_pairs={{0,1},{1,0},{2,3},{3,2},{4,5},{5,4},{6,7},{7,6},{8,9},{9,8},{10,11... | collective-permute-start | bytes 1179656 | tf_op jit(solution)/shard_map/ppermute | solution.py:285

commit v5 on v4

--- a/solution.py
+++ b/solution.py
@@ -33,8 +33,9 @@
 def row_fetches(block, pulses_ref, rows, row_sem):
     width = rows.shape[2]
     return [
-        pltpu.make_async_copy(pulses_ref.at[j, :, pl.ds(block * width, width)], rows.at[j], row_sem.at[j])
-        for j in range(rows.shape[0])
+        pltpu.make_async_copy(
+            pulses_ref.at[pl.ds(j, TEAM), :, pl.ds(block * width, width)], rows.at[pl.ds(j, TEAM)], row_sem.at[j])
+        for j in range(0, rows.shape[0], TEAM)
     ]
 
 
@@ -97,7 +98,10 @@
     blocks = index.shape[3] // (RING * TEAM)
 
     index_copy = pltpu.make_async_copy(index_ref, index, sem.at[0])
-    mat_copies = [pltpu.make_async_copy(bank_ref.at[k], mats.at[k], mat_sem.at[k]) for k in range(kinds)]
+    mat_copies = [
+        pltpu.make_async_copy(bank_ref.at[pl.ds(k, 4)], mats.at[pl.ds(k, 4)], mat_sem.at[k])
+        for k in range(0, kinds, 4)
+    ]
     if joined:
         feeds = [
             pltpu.make_async_copy(part_refs[d], image.at[0, pl.ds(d * TEAM, TEAM)], row_sem.at[d])
@@ -173,7 +177,7 @@
                 stage[place] = merged
 
     index_copy.wait()
-    for level in range(levels if joined else 1):
+    for level in range(levels):
         sort_level(level)
     for copy in feeds:
         copy.wait()
@@ -183,8 +187,6 @@
     for copy in mat_copies:
         copy.wait()
     for level in range(levels):
-        if level + 1 < levels and not joined:
-            sort_level(level + 1)
         merge(level)
 
     half = TEAM // 2

time: 88.4 us -> 88.4 us (level)
  starting transfers between devices: 32.3 us -> 34.3 us
  Pallas kernels: 36.9 us -> 35.9 us
    ppermute x10, starting transfers between devices: 18.1 us -> 19.7 us  [along_sub(): lax.ppermute(value, 'sub', [(i, move(i >> 3, i >> 1 & 3, i & 1)) for i in...]
    pallas_call x2, Pallas kernels: 30.2 us -> 29.3 us  [trees(): pl.pallas_call(functools.partial(tree_kernel, joined, block, levels), in_...]
  transfers between devices with their start and end apart: 20 -> 20, of which waited for: 11 -> 9; matrix products, arithmetic and copies ran while one was open for 0% -> 1% of each run, Pallas kernels for 34% -> 33%
where the time goes in v5:
time: 88.4 us; the launch traced here: 88.3 us
  Pallas kernels  35.9 us (41%)
  starting transfers between devices  34.3 us (39%)
  waiting for transfers between devices  17 us (19%)
    pallas_call x2, Pallas kernels, trees(): pl.pallas_call(functools.partial(tree_kernel, joined, block, levels), in_...  29.3 us
    ppermute x10, starting transfers between devices, along_sub(): lax.ppermute(value, 'sub', [(i, move(i >> 3, i >> 1 & 3, i & 1)) for i in...  19.7 us
    ppermute x10, starting transfers between devices, along_y(): lax.ppermute(value, 'grp', [(i, (i + d) % RING) for i in range(RING)])  14.6 us
    ppermute x10, waiting for transfers between devices, along_sub(): lax.ppermute(value, 'sub', [(i, move(i >> 3, i >> 1 & 3, i & 1)) for i in...  11.8 us
    pallas_call x1, Pallas kernels, start_images(): pl.pallas_call(functools.partial(start_kernel, block), in_specs=[HBM] * 3...  5.38 us
    ppermute x10, waiting for transfers between devices, along_y(): lax.ppermute(value, 'grp', [(i, (i + d) % RING) for i in range(RING)])  5.18 us
  transfers between devices with their start and end apart: 20, of which 9 were waited for; matrix products, arithmetic and copies ran while one was open for 1% of the time, Pallas kernels for 33%

profile of v5, /device:TPU:1, one launch (start us, length us, event | category | flops | bytes accessed | tf_op | source)
XLA Modules:
  0.0 88.3 jit_solution(14181113464809781940)
XLA Ops:
  0.0 5.4 %start.1 = (bf16[8,48,512]{2,1,0:T(8,128)(2,1)S(1)}, bf16[8,48,512]{2,1,0:T(8,128)(2,1)S(1)}, bf16[8,48,512]{2,1,0:T(8,128)(2,1)S(1)}, bf16[8,48,512]{2,1,0:T(8,128)(2,1)S(1)}) custom-call(s32[2,32]{1,0:T(2,128)} %bitcast.55, bf16[32,128,1024]{2,1,0:T(8,128)(2,1)} %bitcast.53, bf16[32,48,256]{2,1,0:T(8,128)(2,1)} %refs_2_.1), custom_call_target="tpu_custom_call" | custom-call | flops 400000000 | bytes 7340032 | tf_op jit(solution)/shard_map/start/pallas_call | solution.py:66
  5.4 2.5 %collective-permute-start.3 = (bf16[8,48,512]{2,1,0:T(8,128)(2,1)S(1)}, bf16[8,48,512]{2,1,0:T(8,128)(2,1)S(1)}, u32[]{:S(2)}, u32[]{:S(2)}) collective-permute-start(bf16[8,48,512]{2,1,0:T(8,128)(2,1)S(1)} %get-tuple-element.40), channel_id=1, source_target_pairs={{0,8},{1,9},{2,10},{3,11},{4,12},{5,13},{6,14},{7,15},{8,16},{9,17... | collective-permute-start | bytes 1179656 | tf_op jit(solution)/shard_map/ppermute | solution.py:287
  7.9 3.3 %collective-permute-start.4 = (bf16[8,48,512]{2,1,0:T(8,128)(2,1)S(1)}, bf16[8,48,512]{2,1,0:T(8,128)(2,1)S(1)}, u32[]{:S(2)}, u32[]{:S(2)}) collective-permute-start(bf16[8,48,512]{2,1,0:T(8,128)(2,1)S(1)} %get-tuple-element.41), channel_id=1, source_target_pairs={{0,16},{1,17},{2,18},{3,19},{4,20},{5,21},{6,22},{7,23},{8,24},{9,... | collective-permute-start | bytes 1179656 | tf_op jit(solution)/shard_map/ppermute | solution.py:287
  12.0 15.3 %trees.1 = (bf16[8,48,512]{2,1,0:T(8,128)(2,1)S(1)}, bf16[8,48,512]{2,1,0:T(8,128)(2,1)S(1)}, bf16[8,48,512]{2,1,0:T(8,128)(2,1)S(1)}, bf16[8,48,512]{2,1,0:T(8,128)(2,1)S(1)}) custom-call(s32[2,32]{1,0:T(2,128)} %bitcast.56, bf16[32,128,1024]{2,1,0:T(8,128)(2,1)} %bitcast.54, bf16[32,48,256]{2,1,0:T(8,128)(2,1)} %refs_2_.1, ...), custom_call_target="tpu_custom_call" | custom-call | flops 8999999488 | bytes 11534336 | tf_op jit(solution)/shard_map/trees/pallas_call | solution.py:234
  27.3 1.6 %collective-permute-start = (bf16[8,48,512]{2,1,0:T(8,128)(2,1)S(1)}, bf16[8,48,512]{2,1,0:T(8,128)(2,1)S(1)}, u32[]{:S(2)}, u32[]{:S(2)}) collective-permute-start(bf16[8,48,512]{2,1,0:T(8,128)(2,1)S(1)} %get-tuple-element.37), channel_id=1, source_target_pairs={{0,32},{32,64},{64,96},{96,0},{1,33},{33,65},{65,97},{97,1},{2,34}... | collective-permute-start | bytes 1179656 | tf_op jit(solution)/shard_map/ppermute | solution.py:284
  28.9 1.3 %collective-permute-start.1 = (bf16[8,48,512]{2,1,0:T(8,128)(2,1)S(1)}, bf16[8,48,512]{2,1,0:T(8,128)(2,1)S(1)}, u32[]{:S(2)}, u32[]{:S(2)}) collective-permute-start(bf16[8,48,512]{2,1,0:T(8,128)(2,1)S(1)} %get-tuple-element.38), channel_id=1, source_target_pairs={{0,64},{32,96},{64,0},{96,32},{1,65},{33,97},{65,1},{97,33},{2,66}... | collective-permute-start | bytes 1179656 | tf_op jit(solution)/shard_map/ppermute | solution.py:284
  30.2 1.3 %collective-permute-start.2 = (bf16[8,48,512]{2,1,0:T(8,128)(2,1)S(1)}, bf16[8,48,512]{2,1,0:T(8,128)(2,1)S(1)}, u32[]{:S(2)}, u32[]{:S(2)}) collective-permute-start(bf16[8,48,512]{2,1,0:T(8,128)(2,1)S(1)} %get-tuple-element.39), channel_id=1, source_target_pairs={{0,96},{32,0},{64,32},{96,64},{1,97},{33,1},{65,33},{97,65},{2,98}... | collective-permute-start | bytes 1179656 | tf_op jit(solution)/shard_map/ppermute | solution.py:284
  31.6 14.0 %joined_trees.1 = (bf16[2,4,48,512]{3,2,1,0:T(8,128)(2,1)S(1)}, bf16[2,4,48,512]{3,2,1,0:T(8,128)(2,1)S(1)}, bf16[4,48,512]{2,1,0:T(8,128)(2,1)S(1)}, bf16[4,48,...) custom-call(bf16[8,48,512]{2,1,0:T(8,128)(2,1)S(1)} %get-tuple-element.35.refs_3_.refs_0_, ...), custom_call_target="tpu_custom_call" | custom-call | flops 8999999488 | bytes 11534336 | tf_op jit(solution)/shard_map/joined_trees/pallas_call | solution.py:234
  46.6 1.8 %collective-permute-start.7 = (bf16[2,4,48,512]{3,2,1,0:T(8,128)(2,1)S(1)}, bf16[2,4,48,512]{3,2,1,0:T(8,128)(2,1)S(1)}, u32[]{:S(2)}, u32[]{:S(2)}) collective-permute-start(bf16[2,4,48,512]{3,2,1,0:T(8,128)(2,1)S(1)} %get-tuple-element.46), channel_id=1, source_target_pairs={{0,96},{32,0},{64,32},{96,64},{1,97},{33,1},{65,33},{97,65},{2,98}... | collective-permute-start | bytes 1179656 | tf_op jit(solution)/shard_map/ppermute | solution.py:284
  49.4 1.1 %collective-permute-start.8 = (bf16[2,48,512]{2,1,0:T(8,128)(2,1)S(1)}, bf16[2,48,512]{2,1,0:T(8,128)(2,1)S(1)}, u32[]{:S(2)}, u32[]{:S(2)}) collective-permute-start(bf16[2,48,512]{2,1,0:T(8,128)(2,1)S(1)} %get-tuple-element.67), channel_id=1, source_target_pairs={{0,8},{1,9},{2,10},{3,11},{4,12},{5,13},{6,14},{7,15},{8,16},{9,17... | collective-permute-start | bytes 294920 | tf_op jit(solution)/shard_map/ppermute | solution.py:287
  50.5 1.7 %collective-permute-start.9 = (bf16[2,48,512]{2,1,0:T(8,128)(2,1)S(1)}, bf16[2,48,512]{2,1,0:T(8,128)(2,1)S(1)}, u32[]{:S(2)}, u32[]{:S(2)}) collective-permute-start(bf16[2,48,512]{2,1,0:T(8,128)(2,1)S(1)} %get-tuple-element.66), channel_id=1, source_target_pairs={{0,16},{1,17},{2,18},{3,19},{4,20},{5,21},{6,22},{7,23},{8,24},{9,... | collective-permute-start | bytes 294920 | tf_op jit(solution)/shard_map/ppermute | solution.py:287
  52.7 1.7 %collective-permute-done.8 = bf16[2,48,512]{2,1,0:T(8,128)(2,1)S(1)} collective-permute-done((bf16[2,48,512]{2,1,0:T(8,128)(2,1)S(1)}, bf16[2,48,512]{2,1,0:T(8,128)(2,1)S(1)}, u32[]{:S(2)}, u32[]{:S(2)}) %collective-permute-start.8) | collective-permute-done | bytes 98336 | tf_op jit(solution)/shard_map/ppermute | solution.py:287
  54.4 1.1 %collective-permute-done.9 = bf16[2,48,512]{2,1,0:T(8,128)(2,1)S(1)} collective-permute-done((bf16[2,48,512]{2,1,0:T(8,128)(2,1)S(1)}, bf16[2,48,512]{2,1,0:T(8,128)(2,1)S(1)}, u32[]{:S(2)}, u32[]{:S(2)}) %collective-permute-start.9) | collective-permute-done | bytes 98336 | tf_op jit(solution)/shard_map/ppermute | solution.py:287
  55.5 3.6 %collective-permute-start.12 = (bf16[4,48,512]{2,1,0:T(8,128)(2,1)S(1)}, bf16[4,48,512]{2,1,0:T(8,128)(2,1)S(1)}, u32[]{:S(2)}, u32[]{:S(2)}) collective-permute-start(bf16[4,48,512]{2,1,0:T(8,128)(2,1)S(1)} %fusion), channel_id=1, source_target_pairs={{0,96},{32,0},{64,32},{96,64},{1,97},{33,1},{65,33},{97,65},{2,98}... | collective-permute-start | bytes 589832 | tf_op jit(solution)/shard_map/ppermute | solution.py:284
  59.9 3.3 %collective-permute-start.14 = (bf16[2,48,512]{2,1,0:T(8,128)(2,1)S(1)}, bf16[2,48,512]{2,1,0:T(8,128)(2,1)S(1)}, u32[]{:S(2)}, u32[]{:S(2)}) collective-permute-start(bf16[2,48,512]{2,1,0:T(8,128)(2,1)S(1)} %get-tuple-element.80), channel_id=1, source_target_pairs={{0,64},{32,96},{64,0},{96,32},{1,65},{33,97},{65,1},{97,33},{2,66}... | collective-permute-start | bytes 294920 | tf_op jit(solution)/shard_map/ppermute | solution.py:284
  63.2 3.3 %collective-permute-done.13 = bf16[2,48,512]{2,1,0:T(8,128)(2,1)S(1)} collective-permute-done((bf16[2,48,512]{2,1,0:T(8,128)(2,1)S(1)}, bf16[2,48,512]{2,1,0:T(8,128)(2,1)S(1)}, u32[]{:S(2)}, u32[]{:S(2)}) %collective-permute-start.13) | collective-permute-done | bytes 98336 | tf_op jit(solution)/shard_map/ppermute | solution.py:284
  66.5 1.8 %collective-permute-done.14 = bf16[2,48,512]{2,1,0:T(8,128)(2,1)S(1)} collective-permute-done((bf16[2,48,512]{2,1,0:T(8,128)(2,1)S(1)}, bf16[2,48,512]{2,1,0:T(8,128)(2,1)S(1)}, u32[]{:S(2)}, u32[]{:S(2)}) %collective-permute-start.14) | collective-permute-done | bytes 98336 | tf_op jit(solution)/shard_map/ppermute | solution.py:284
  68.6 3.7 %collective-permute-start.18 = (bf16[2,2,48,512]{3,2,0,1:T(8,128)(2,1)S(1)}, bf16[2,2,48,512]{3,2,0,1:T(8,128)(2,1)S(1)}, u32[]{:S(2)}, u32[]{:S(2)}) collective-permute-start(bf16[2,2,48,512]{3,2,0,1:T(8,128)(2,1)S(1)} %pad_maximum_fusion.4), channel_id=1, source_target_pairs={{0,6},{1,7},{2,0},{3,1},{4,2},{5,3},{6,4},{7,5},{8,14},{9,15},{10,... | collective-permute-start | bytes 589832 | tf_op jit(solution)/shard_map/ppermute | solution.py:287
  73.1 3.9 %collective-permute-done.18 = bf16[2,2,48,512]{3,2,0,1:T(8,128)(2,1)S(1)} collective-permute-done((bf16[2,2,48,512]{3,2,0,1:T(8,128)(2,1)S(1)}, bf16[2,2,48,512]{3,2,0,1:T(8,128)(2,1)S(1)}, u32[]{:S(2)}, u32[]{:S(2)}) %collective-permute-start.18) | collective-permute-done | bytes 196640 | tf_op jit(solution)/shard_map/ppermute | solution.py:287
  77.0 1.5 %collective-permute-done.17.refs_2_ = bf16[2,2,48,512]{3,2,1,0:T(8,128)(2,1)S(1)} collective-permute-done((bf16[2,2,48,512]{3,2,1,0:T(8,128)(2,1)S(1)}, bf16[2,2,48,512]{3,2,1,0:T(8,128)(2,1)S(1)}, u32[]{:S(2)}, u32[]{:S(2)}) %collective-permute-start.17) | collective-permute-done | bytes 196640 | tf_op jit(solution)/shard_map/ppermute | solution.py:287
  78.5 1.8 %collective-permute-done.16.refs_1_ = bf16[2,2,48,512]{3,2,1,0:T(8,128)(2,1)S(1)} collective-permute-done((bf16[2,2,48,512]{3,2,1,0:T(8,128)(2,1)S(1)}, bf16[2,2,48,512]{3,2,1,0:T(8,128)(2,1)S(1)}, u32[]{:S(2)}, u32[]{:S(2)}) %collective-permute-start.16) | collective-permute-done | bytes 196640 | tf_op jit(solution)/shard_map/ppermute | solution.py:287
  80.4 5.1 %collective-permute-start.19 = (bf16[4,2,48,512]{3,2,1,0:T(8,128)(2,1)S(1)}, bf16[4,2,48,512]{3,2,1,0:T(8,128)(2,1)S(1)}, u32[]{:S(2)}, u32[]{:S(2)}) collective-permute-start(bf16[4,2,48,512]{3,2,1,0:T(8,128)(2,1)S(1)} %pad_maximum_fusion), channel_id=1, source_target_pairs={{0,1},{1,0},{2,3},{3,2},{4,5},{5,4},{6,7},{7,6},{8,9},{9,8},{10,11... | collective-permute-start | bytes 1179656 | tf_op jit(solution)/shard_map/ppermute | solution.py:287
  85.6 1.3 %collective-permute-done.19.refs_4_ = bf16[4,2,48,512]{3,2,1,0:T(8,128)(2,1)S(1)} collective-permute-done((bf16[4,2,48,512]{3,2,1,0:T(8,128)(2,1)S(1)}, bf16[4,2,48,512]{3,2,1,0:T(8,128)(2,1)S(1)}, u32[]{:S(2)}, u32[]{:S(2)}) %collective-permute-start.19) | collective-permute-done | bytes 393248 | tf_op jit(solution)/shard_map/ppermute | solution.py:287
  86.9 1.2 %lay.1 = bf16[48,8192]{1,0:T(8,128)(2,1)} custom-call(bf16[2,2,48,512]{3,2,1,0:T(8,128)(2,1)S(1)} %pad_maximum_fusion.1.refs_0_, bf16[2,2,48,512]{3,2,1,0:T(8,128)(2,1)S(1)} %collective-permute-done.16.refs_1_, bf16[2,2,48,512]{3,2,1,0:T(8,128)(2,1)S(1)} %collective-permute-done.17.refs_2_, bf16[2,2,48,512]{3,2,1,0:T(8,128)(2,1)S(1)} %copy.8.refs_3_, ...), custom_call_target="tpu_custom_call" | custom-call | tf_op jit(solution)/shard_map/lay/pallas_call | solution.py:325
  (36 shorter events, 5.3 us)
Async XLA Ops:
  5.4 24.8 %collective-permute-start.3 = (bf16[8,48,512]{2,1,0:T(8,128)(2,1)S(1)}, bf16[8,48,512]{2,1,0:T(8,128)(2,1)S(1)}, u32[]{:S(2)}, u32[]{:S(2)}) collective-permute-start(bf16[8,48,512]{2,1,0:T(8,128)(2,1)S(1)} %get-tuple-element.40), channel_id=1, source_target_pairs={{0,8},{1,9},{2,10},{3,11},{4,12},{5,13},{6,14},{7,15},{8,16},{9,17... | collective-permute-start | bytes 1179656 | tf_op jit(solution)/shard_map/ppermute | solution.py:287
  7.9 23.6 %collective-permute-start.4 = (bf16[8,48,512]{2,1,0:T(8,128)(2,1)S(1)}, bf16[8,48,512]{2,1,0:T(8,128)(2,1)S(1)}, u32[]{:S(2)}, u32[]{:S(2)}) collective-permute-start(bf16[8,48,512]{2,1,0:T(8,128)(2,1)S(1)} %get-tuple-element.41), channel_id=1, source_target_pairs={{0,16},{1,17},{2,18},{3,19},{4,20},{5,21},{6,22},{7,23},{8,24},{9,... | collective-permute-start | bytes 1179656 | tf_op jit(solution)/shard_map/ppermute | solution.py:287
  11.2 20.3 %collective-permute-start.5 = (bf16[8,48,512]{2,1,0:T(8,128)(2,1)S(1)}, bf16[8,48,512]{2,1,0:T(8,128)(2,1)S(1)}, u32[]{:S(2)}, u32[]{:S(2)}) collective-permute-start(bf16[8,48,512]{2,1,0:T(8,128)(2,1)S(1)} %get-tuple-element.42), channel_id=1, source_target_pairs={{0,24},{1,25},{2,26},{3,27},{4,28},{5,29},{6,30},{7,31},{8,0},{9,1... | collective-permute-start | bytes 1179656 | tf_op jit(solution)/shard_map/ppermute | solution.py:287
  27.3 21.0 %collective-permute-start = (bf16[8,48,512]{2,1,0:T(8,128)(2,1)S(1)}, bf16[8,48,512]{2,1,0:T(8,128)(2,1)S(1)}, u32[]{:S(2)}, u32[]{:S(2)}) collective-permute-start(bf16[8,48,512]{2,1,0:T(8,128)(2,1)S(1)} %get-tuple-element.37), channel_id=1, source_target_pairs={{0,32},{32,64},{64,96},{96,0},{1,33},{33,65},{65,97},{97,1},{2,34}... | collective-permute-start | bytes 1179656 | tf_op jit(solution)/shard_map/ppermute | solution.py:284
  28.9 19.4 %collective-permute-start.1 = (bf16[8,48,512]{2,1,0:T(8,128)(2,1)S(1)}, bf16[8,48,512]{2,1,0:T(8,128)(2,1)S(1)}, u32[]{:S(2)}, u32[]{:S(2)}) collective-permute-start(bf16[8,48,512]{2,1,0:T(8,128)(2,1)S(1)} %get-tuple-element.38), channel_id=1, source_target_pairs={{0,64},{32,96},{64,0},{96,32},{1,65},{33,97},{65,1},{97,33},{2,66}... | collective-permute-start | bytes 1179656 | tf_op jit(solution)/shard_map/ppermute | solution.py:284
  30.2 18.1 %collective-permute-start.2 = (bf16[8,48,512]{2,1,0:T(8,128)(2,1)S(1)}, bf16[8,48,512]{2,1,0:T(8,128)(2,1)S(1)}, u32[]{:S(2)}, u32[]{:S(2)}) collective-permute-start(bf16[8,48,512]{2,1,0:T(8,128)(2,1)S(1)} %get-tuple-element.39), channel_id=1, source_target_pairs={{0,96},{32,0},{64,32},{96,64},{1,97},{33,1},{65,33},{97,65},{2,98}... | collective-permute-start | bytes 1179656 | tf_op jit(solution)/shard_map/ppermute | solution.py:284
  45.6 9.9 %collective-permute-start.6 = (bf16[2,4,48,512]{3,2,1,0:T(8,128)(2,1)S(1)}, bf16[2,4,48,512]{3,2,1,0:T(8,128)(2,1)S(1)}, u32[]{:S(2)}, u32[]{:S(2)}) collective-permute-start(bf16[2,4,48,512]{3,2,1,0:T(8,128)(2,1)S(1)} %get-tuple-element.45), channel_id=1, source_target_pairs={{0,32},{32,64},{64,96},{96,0},{1,33},{33,65},{65,97},{97,1},{2,34}... | collective-permute-start | bytes 1179656 | tf_op jit(solution)/shard_map/ppermute | solution.py:284
  46.6 8.9 %collective-permute-start.7 = (bf16[2,4,48,512]{3,2,1,0:T(8,128)(2,1)S(1)}, bf16[2,4,48,512]{3,2,1,0:T(8,128)(2,1)S(1)}, u32[]{:S(2)}, u32[]{:S(2)}) collective-permute-start(bf16[2,4,48,512]{3,2,1,0:T(8,128)(2,1)S(1)} %get-tuple-element.46), channel_id=1, source_target_pairs={{0,96},{32,0},{64,32},{96,64},{1,97},{33,1},{65,33},{97,65},{2,98}... | collective-permute-start | bytes 1179656 | tf_op jit(solution)/shard_map/ppermute | solution.py:284
  48.5 4.1 %collective-permute-start.10 = (bf16[2,48,512]{2,1,0:T(8,128)(2,1)S(1)}, bf16[2,48,512]{2,1,0:T(8,128)(2,1)S(1)}, u32[]{:S(2)}, u32[]{:S(2)}) collective-permute-start(bf16[2,48,512]{2,1,0:T(8,128)(2,1)S(1)} %get-tuple-element.65), channel_id=1, source_target_pairs={{0,24},{1,25},{2,26},{3,27},{4,28},{5,29},{6,30},{7,31},{8,0},{9,1... | collective-permute-start | bytes 294920 | tf_op jit(solution)/shard_map/ppermute | solution.py:287
  49.4 5.0 %collective-permute-start.8 = (bf16[2,48,512]{2,1,0:T(8,128)(2,1)S(1)}, bf16[2,48,512]{2,1,0:T(8,128)(2,1)S(1)}, u32[]{:S(2)}, u32[]{:S(2)}) collective-permute-start(bf16[2,48,512]{2,1,0:T(8,128)(2,1)S(1)} %get-tuple-element.67), channel_id=1, source_target_pairs={{0,8},{1,9},{2,10},{3,11},{4,12},{5,13},{6,14},{7,15},{8,16},{9,17... | collective-permute-start | bytes 294920 | tf_op jit(solution)/shard_map/ppermute | solution.py:287
  50.5 5.0 %collective-permute-start.9 = (bf16[2,48,512]{2,1,0:T(8,128)(2,1)S(1)}, bf16[2,48,512]{2,1,0:T(8,128)(2,1)S(1)}, u32[]{:S(2)}, u32[]{:S(2)}) collective-permute-start(bf16[2,48,512]{2,1,0:T(8,128)(2,1)S(1)} %get-tuple-element.66), channel_id=1, source_target_pairs={{0,16},{1,17},{2,18},{3,19},{4,20},{5,21},{6,22},{7,23},{8,24},{9,... | collective-permute-start | bytes 294920 | tf_op jit(solution)/shard_map/ppermute | solution.py:287
  55.5 12.9 %collective-permute-start.12 = (bf16[4,48,512]{2,1,0:T(8,128)(2,1)S(1)}, bf16[4,48,512]{2,1,0:T(8,128)(2,1)S(1)}, u32[]{:S(2)}, u32[]{:S(2)}) collective-permute-start(bf16[4,48,512]{2,1,0:T(8,128)(2,1)S(1)} %fusion), channel_id=1, source_target_pairs={{0,96},{32,0},{64,32},{96,64},{1,97},{33,1},{65,33},{97,65},{2,98}... | collective-permute-start | bytes 589832 | tf_op jit(solution)/shard_map/ppermute | solution.py:284
  59.1 9.2 %collective-permute-start.11 = (bf16[4,48,512]{2,1,0:T(8,128)(2,1)S(1)}, bf16[4,48,512]{2,1,0:T(8,128)(2,1)S(1)}, u32[]{:S(2)}, u32[]{:S(2)}) collective-permute-start(bf16[4,48,512]{2,1,0:T(8,128)(2,1)S(1)} %fusion.1), channel_id=1, source_target_pairs={{0,32},{32,64},{64,96},{96,0},{1,33},{33,65},{65,97},{97,1},{2,34}... | collective-permute-start | bytes 589832 | tf_op jit(solution)/shard_map/ppermute | solution.py:284
  59.3 7.3 %collective-permute-start.13 = (bf16[2,48,512]{2,1,0:T(8,128)(2,1)S(1)}, bf16[2,48,512]{2,1,0:T(8,128)(2,1)S(1)}, u32[]{:S(2)}, u32[]{:S(2)}) collective-permute-start(bf16[2,48,512]{2,1,0:T(8,128)(2,1)S(1)} %get-tuple-element.81), channel_id=1, source_target_pairs={{0,32},{32,64},{64,96},{96,0},{1,33},{33,65},{65,97},{97,1},{2,34}... | collective-permute-start | bytes 294920 | tf_op jit(solution)/shard_map/ppermute | solution.py:284
  59.9 8.4 %collective-permute-start.14 = (bf16[2,48,512]{2,1,0:T(8,128)(2,1)S(1)}, bf16[2,48,512]{2,1,0:T(8,128)(2,1)S(1)}, u32[]{:S(2)}, u32[]{:S(2)}) collective-permute-start(bf16[2,48,512]{2,1,0:T(8,128)(2,1)S(1)} %get-tuple-element.80), channel_id=1, source_target_pairs={{0,64},{32,96},{64,0},{96,32},{1,65},{33,97},{65,1},{97,33},{2,66}... | collective-permute-start | bytes 294920 | tf_op jit(solution)/shard_map/ppermute | solution.py:284
  63.2 5.2 %collective-permute-start.15 = (bf16[2,48,512]{2,1,0:T(8,128)(2,1)S(1)}, bf16[2,48,512]{2,1,0:T(8,128)(2,1)S(1)}, u32[]{:S(2)}, u32[]{:S(2)}) collective-permute-start(bf16[2,48,512]{2,1,0:T(8,128)(2,1)S(1)} %get-tuple-element.79), channel_id=1, source_target_pairs={{0,96},{32,0},{64,32},{96,64},{1,97},{33,1},{65,33},{97,65},{2,98}... | collective-permute-start | bytes 294920 | tf_op jit(solution)/shard_map/ppermute | solution.py:284
  68.6 8.4 %collective-permute-start.18 = (bf16[2,2,48,512]{3,2,0,1:T(8,128)(2,1)S(1)}, bf16[2,2,48,512]{3,2,0,1:T(8,128)(2,1)S(1)}, u32[]{:S(2)}, u32[]{:S(2)}) collective-permute-start(bf16[2,2,48,512]{3,2,0,1:T(8,128)(2,1)S(1)} %pad_maximum_fusion.4), channel_id=1, source_target_pairs={{0,6},{1,7},{2,0},{3,1},{4,2},{5,3},{6,4},{7,5},{8,14},{9,15},{10,... | collective-permute-start | bytes 589832 | tf_op jit(solution)/shard_map/ppermute | solution.py:287
  72.3 6.2 %collective-permute-start.17 = (bf16[2,2,48,512]{3,2,1,0:T(8,128)(2,1)S(1)}, bf16[2,2,48,512]{3,2,1,0:T(8,128)(2,1)S(1)}, u32[]{:S(2)}, u32[]{:S(2)}) collective-permute-start(bf16[2,2,48,512]{3,2,1,0:T(8,128)(2,1)S(1)} %pad_maximum_fusion.3), channel_id=1, source_target_pairs={{0,4},{1,5},{2,6},{3,7},{4,0},{5,1},{6,2},{7,3},{8,12},{9,13},{10,... | collective-permute-start | bytes 589832 | tf_op jit(solution)/shard_map/ppermute | solution.py:287
  72.4 7.9 %collective-permute-start.16 = (bf16[2,2,48,512]{3,2,1,0:T(8,128)(2,1)S(1)}, bf16[2,2,48,512]{3,2,1,0:T(8,128)(2,1)S(1)}, u32[]{:S(2)}, u32[]{:S(2)}) collective-permute-start(bf16[2,2,48,512]{3,2,1,0:T(8,128)(2,1)S(1)} %pad_maximum_fusion.2), channel_id=1, source_target_pairs={{0,2},{1,3},{2,4},{3,5},{4,6},{5,7},{6,0},{7,1},{8,10},{9,11},{10,... | collective-permute-start | bytes 589832 | tf_op jit(solution)/shard_map/ppermute | solution.py:287
  80.4 6.5 %collective-permute-start.19 = (bf16[4,2,48,512]{3,2,1,0:T(8,128)(2,1)S(1)}, bf16[4,2,48,512]{3,2,1,0:T(8,128)(2,1)S(1)}, u32[]{:S(2)}, u32[]{:S(2)}) collective-permute-start(bf16[4,2,48,512]{3,2,1,0:T(8,128)(2,1)S(1)} %pad_maximum_fusion), channel_id=1, source_target_pairs={{0,1},{1,0},{2,3},{3,2},{4,5},{5,4},{6,7},{7,6},{8,9},{9,8},{10,11... | collective-permute-start | bytes 1179656 | tf_op jit(solution)/shard_map/ppermute | solution.py:287
